TPU v7x, 256 devices: a whole 4x4x8 slice. The times are simulated.
256 devices in a mesh: tm: 16 (over x_hi, z), tile: 16 (over x_lo, y, core).
Axes of the slice: x: 4 (x_hi: 2, x_lo: 2; x = x_hi * 2 + x_lo), y: 4, z: 8, core: 2. Of those that a mesh axis runs over, the one named last changes fastest.
Arguments:
- initial: float32 [3, 512, 512], P(None, 'tile'), may hold values from -6 to 6
- rotation: float32 [512, 512], P('tile'), may hold values from -0.15 to 0.15
- seam_flip: int32 [16], replicated, may hold values from 0 to 1
Outputs:
- slice_ends: float32 [16, 3, 512, 512], P('tm', None, 'tile')
All inputs are finite; a program needn't handle non-finite values.
Results may differ from a plain program's by a relative error of at most 0.0001.
Values sent between devices are 32-bit elements; how exact they have to be, the bound alone decides.
A program may use at most 64 MiB of HBM per device.

v0:
```python
import jax
import jax.numpy as jnp
from jax import lax
from jax.sharding import PartitionSpec as P

FSTEPS = 8
CSTEPS = 2
FACTOR = 4
SWEEPS = 2


courant = 0.9


def with_halo(x, sides, width):
    for axis, dim in sides:
        size, length = (lax.axis_size(axis), x.shape[dim])
        up = [(i, (i + 1) % size) for i in range(size)]
        down = [(j, i) for i, j in up]
        last = lax.slice_in_dim(x, length - width, length, axis=dim)
        initial = lax.slice_in_dim(x, 0, width, axis=dim)
        before = lax.ppermute(last, axis, up)
        after = lax.ppermute(initial, axis, down)
        x = jnp.concatenate([before, x, after], axis=dim)
    return x


def passed_along(block, axis, distance):
    devices = range(lax.axis_size(axis))
    route = [(i - distance, i) for i in devices if i - distance in devices]
    return lax.ppermute(block, axis, route)


def reflect(rim, flag, field_signs):
    return jnp.where(flag, field_signs * jnp.flip(rim, -1), rim)


def advance(extended, rotation_rate):
    height, flow_across, flow_along = (extended[0], extended[1], extended[2])
    across_slope = (flow_across[..., 2:, :] - flow_across[..., :-2, :]) * 0.5
    along_mid = flow_along[..., 1:-1, :]
    along_slope = (jnp.roll(along_mid, -1, -1) - jnp.roll(along_mid, 1, -1)) * 0.5
    height_new = height[..., 1:-1, :] - courant * (across_slope + along_slope)
    height_core = height_new[..., 1:-1, :]
    height_across = (height_new[..., 2:, :] - height_new[..., :-2, :]) * 0.5
    height_along = (jnp.roll(height_core, -1, -1) - jnp.roll(height_core, 1, -1)) * 0.5
    across_core = flow_across[..., 2:-2, :]
    along_core = flow_along[..., 2:-2, :]
    across_new = across_core + rotation_rate * along_core - courant * height_across
    along_new = along_core - rotation_rate * across_new - courant * height_along
    return jnp.stack([height_core, across_new, along_new])


def restrict(field_in):
    field_shape = field_in.shape
    grouped = field_in.reshape(
        field_shape[:-2] + (field_shape[-2] // FACTOR, FACTOR, field_shape[-1] // FACTOR, FACTOR)
    )
    return jnp.mean(grouped, axis=(-3, -1))


def prolong(field_in):
    return jnp.repeat(jnp.repeat(field_in, FACTOR, axis=-2), FACTOR, axis=-1)


def orient(extended, rim_width, lower_flip, upper_flip, field_signs):
    below = reflect(extended[:, :rim_width], lower_flip, field_signs)
    above = reflect(extended[:, -rim_width:], upper_flip, field_signs)
    return jnp.concatenate([below, extended[:, rim_width:-rim_width], above], axis=1)


def body(initial, rotation, seam_flip):
    tile_count = lax.axis_size("tile")
    tile_index = lax.axis_index("tile")
    positions = jnp.arange(tile_count, dtype=jnp.int32)
    lower_flip = jnp.sum(jnp.where(positions == tile_index, seam_flip, 0)) != 0
    upper_flip = jnp.sum(jnp.where(positions == (tile_index + 1) % tile_count, seam_flip, 0)) != 0
    field_signs = jnp.array([1.0, 1.0, -1.0], jnp.float32).reshape(3, 1, 1)
    rate_signs = jnp.array([-1.0], jnp.float32).reshape(1, 1, 1)
    rim_coarse = 2 * CSTEPS
    rate_wide = with_halo((FACTOR * restrict(rotation))[None], (("tile", 1),), rim_coarse)
    coarse_rate = orient(rate_wide, rim_coarse, lower_flip, upper_flip, rate_signs)[0]

    def coarse(state):
        extended = with_halo(state, (("tile", 1),), rim_coarse)
        extended = orient(extended, rim_coarse, lower_flip, upper_flip, field_signs)
        for substep in range(CSTEPS):
            margin_rows = 2 + 2 * substep
            extended = advance(
                extended, coarse_rate[margin_rows : coarse_rate.shape[0] - margin_rows, :]
            )
        return extended

    def fine_run(state):
        for substep in range(FSTEPS):
            extended = with_halo(state, (("tile", 1),), 2)
            state = advance(orient(extended, 2, lower_flip, upper_flip, field_signs), rotation)
        return state

    slice_index = lax.axis_index("tm")
    slice_count = lax.axis_size("tm")
    anchor = restrict(initial)
    coarse_old = coarse(anchor)
    current = fine_run(initial)
    for sweep_index in range(SWEEPS):
        if sweep_index > 0:
            current = fine_run(restart_state)
        coarse_fine = restrict(current)
        offset = coarse_fine - coarse_old
        last_sweep = sweep_index + 1 == SWEEPS

        def chain_turn(turn_index, inbound):
            advanced = coarse(inbound) + offset
            arrived = passed_along(advanced, "tm", 1)
            return jnp.where(slice_index == turn_index + 1, arrived, inbound)

        inbound = lax.fori_loop(0, slice_count - 1, chain_turn, anchor)
        coarse_end = coarse(inbound) + offset
        coarse_old = coarse_end - offset
        if not last_sweep:
            restart_state = passed_along(current + prolong(coarse_end - coarse_fine), "tm", 1)
            restart_state = jnp.where(slice_index == 0, initial, restart_state)
    return (current + prolong(coarse_end - coarse_fine))[None]


def solution(mesh):
    in_specs = (P(None, "tile", None), P("tile", None), P())
    out_specs = P("tm", None, "tile", None)
    return jax.shard_map(body, mesh=mesh, in_specs=in_specs, out_specs=out_specs, check_vma=False)
```

profile of v0, /device:TPU:4, one launch (start us, length us, event | category | flops | bytes accessed | tf_op | source)
XLA Modules:
  0.0 645.4 jit_solution(2292255776354186001)
XLA Ops:
  0.0 8.7 %reshape.351 = f32[3,8,4,128,4]{4,3,2,1,0:T(8,128)} reshape(f32[3,32,512]{2,1,0:T(8,128)} %param.9) | data formatting | bytes 393216 | tf_op jit(solution)/shard_map/reshape | solution.py:56
  86.3 235.5 %while.34 = (s32[]{:T(128)}, f32[3,8,128]{2,1,0:T(8,128)S(1)}, s32[]{:T(128)}, pred[]{:T(512)}, pred[]{:T(512)}, /*index=5*/f32[16,128]{1,0:T(8,128)S(1)}, f32[3,8,128]{2,1,0:T(8,128)S(1)}, s32[]{:T(128)}, f32[3]{0:T(128)S(1)}) while((s32[]{:T(128)}, f32[3,8,128]{2,1,0:T(8,128)S(1)}, s32[]{:T(128)}, pred[]{:T(512)}, pred[]{:T(512)}, ...), condition=%wide.region_6.7_spmd.clone, body=%wide.region_5.6_spmd.clone.sunk | while | flops 82947 | bytes 585965 | solution.py:117
  110.6 7.3 %collective-permute-done.2 = f32[3,8,128]{2,1,0:T(8,128)S(1)} collective-permute-done((f32[3,8,128]{2,1,0:T(8,128)S(1)}, f32[3,8,128]{2,1,0:T(8,128)S(1)}, u32[]{:S(2)}, u32[]{:S(2)}) %collective-permute-start.2) | collective-permute-done | bytes 12320 | tf_op jit(solution)/shard_map/while/body/eval_jaxpr/ppermute | solution.py:31
  126.3 7.3 %collective-permute-done.2 = f32[3,8,128]{2,1,0:T(8,128)S(1)} collective-permute-done((f32[3,8,128]{2,1,0:T(8,128)S(1)}, f32[3,8,128]{2,1,0:T(8,128)S(1)}, u32[]{:S(2)}, u32[]{:S(2)}) %collective-permute-start.2) | collective-permute-done | bytes 12320 | tf_op jit(solution)/shard_map/while/body/eval_jaxpr/ppermute | solution.py:31
  142.0 7.3 %collective-permute-done.2 = f32[3,8,128]{2,1,0:T(8,128)S(1)} collective-permute-done((f32[3,8,128]{2,1,0:T(8,128)S(1)}, f32[3,8,128]{2,1,0:T(8,128)S(1)}, u32[]{:S(2)}, u32[]{:S(2)}) %collective-permute-start.2) | collective-permute-done | bytes 12320 | tf_op jit(solution)/shard_map/while/body/eval_jaxpr/ppermute | solution.py:31
  157.6 7.3 %collective-permute-done.2 = f32[3,8,128]{2,1,0:T(8,128)S(1)} collective-permute-done((f32[3,8,128]{2,1,0:T(8,128)S(1)}, f32[3,8,128]{2,1,0:T(8,128)S(1)}, u32[]{:S(2)}, u32[]{:S(2)}) %collective-permute-start.2) | collective-permute-done | bytes 12320 | tf_op jit(solution)/shard_map/while/body/eval_jaxpr/ppermute | solution.py:31
  173.3 7.3 %collective-permute-done.2 = f32[3,8,128]{2,1,0:T(8,128)S(1)} collective-permute-done((f32[3,8,128]{2,1,0:T(8,128)S(1)}, f32[3,8,128]{2,1,0:T(8,128)S(1)}, u32[]{:S(2)}, u32[]{:S(2)}) %collective-permute-start.2) | collective-permute-done | bytes 12320 | tf_op jit(solution)/shard_map/while/body/eval_jaxpr/ppermute | solution.py:31
  189.0 7.3 %collective-permute-done.2 = f32[3,8,128]{2,1,0:T(8,128)S(1)} collective-permute-done((f32[3,8,128]{2,1,0:T(8,128)S(1)}, f32[3,8,128]{2,1,0:T(8,128)S(1)}, u32[]{:S(2)}, u32[]{:S(2)}) %collective-permute-start.2) | collective-permute-done | bytes 12320 | tf_op jit(solution)/shard_map/while/body/eval_jaxpr/ppermute | solution.py:31
  204.7 7.3 %collective-permute-done.2 = f32[3,8,128]{2,1,0:T(8,128)S(1)} collective-permute-done((f32[3,8,128]{2,1,0:T(8,128)S(1)}, f32[3,8,128]{2,1,0:T(8,128)S(1)}, u32[]{:S(2)}, u32[]{:S(2)}) %collective-permute-start.2) | collective-permute-done | bytes 12320 | tf_op jit(solution)/shard_map/while/body/eval_jaxpr/ppermute | solution.py:31
  220.4 7.3 %collective-permute-done.2 = f32[3,8,128]{2,1,0:T(8,128)S(1)} collective-permute-done((f32[3,8,128]{2,1,0:T(8,128)S(1)}, f32[3,8,128]{2,1,0:T(8,128)S(1)}, u32[]{:S(2)}, u32[]{:S(2)}) %collective-permute-start.2) | collective-permute-done | bytes 12320 | tf_op jit(solution)/shard_map/while/body/eval_jaxpr/ppermute | solution.py:31
  236.1 7.3 %collective-permute-done.2 = f32[3,8,128]{2,1,0:T(8,128)S(1)} collective-permute-done((f32[3,8,128]{2,1,0:T(8,128)S(1)}, f32[3,8,128]{2,1,0:T(8,128)S(1)}, u32[]{:S(2)}, u32[]{:S(2)}) %collective-permute-start.2) | collective-permute-done | bytes 12320 | tf_op jit(solution)/shard_map/while/body/eval_jaxpr/ppermute | solution.py:31
  251.8 7.3 %collective-permute-done.2 = f32[3,8,128]{2,1,0:T(8,128)S(1)} collective-permute-done((f32[3,8,128]{2,1,0:T(8,128)S(1)}, f32[3,8,128]{2,1,0:T(8,128)S(1)}, u32[]{:S(2)}, u32[]{:S(2)}) %collective-permute-start.2) | collective-permute-done | bytes 12320 | tf_op jit(solution)/shard_map/while/body/eval_jaxpr/ppermute | solution.py:31
  267.4 7.3 %collective-permute-done.2 = f32[3,8,128]{2,1,0:T(8,128)S(1)} collective-permute-done((f32[3,8,128]{2,1,0:T(8,128)S(1)}, f32[3,8,128]{2,1,0:T(8,128)S(1)}, u32[]{:S(2)}, u32[]{:S(2)}) %collective-permute-start.2) | collective-permute-done | bytes 12320 | tf_op jit(solution)/shard_map/while/body/eval_jaxpr/ppermute | solution.py:31
  283.1 7.3 %collective-permute-done.2 = f32[3,8,128]{2,1,0:T(8,128)S(1)} collective-permute-done((f32[3,8,128]{2,1,0:T(8,128)S(1)}, f32[3,8,128]{2,1,0:T(8,128)S(1)}, u32[]{:S(2)}, u32[]{:S(2)}) %collective-permute-start.2) | collective-permute-done | bytes 12320 | tf_op jit(solution)/shard_map/while/body/eval_jaxpr/ppermute | solution.py:31
  298.8 7.3 %collective-permute-done.2 = f32[3,8,128]{2,1,0:T(8,128)S(1)} collective-permute-done((f32[3,8,128]{2,1,0:T(8,128)S(1)}, f32[3,8,128]{2,1,0:T(8,128)S(1)}, u32[]{:S(2)}, u32[]{:S(2)}) %collective-permute-start.2) | collective-permute-done | bytes 12320 | tf_op jit(solution)/shard_map/while/body/eval_jaxpr/ppermute | solution.py:31
  314.5 7.3 %collective-permute-done.2 = f32[3,8,128]{2,1,0:T(8,128)S(1)} collective-permute-done((f32[3,8,128]{2,1,0:T(8,128)S(1)}, f32[3,8,128]{2,1,0:T(8,128)S(1)}, u32[]{:S(2)}, u32[]{:S(2)}) %collective-permute-start.2) | collective-permute-done | bytes 12320 | tf_op jit(solution)/shard_map/while/body/eval_jaxpr/ppermute | solution.py:31
  330.8 9.2 %collective-permute-done.28 = f32[3,32,512]{2,1,0:T(8,128)S(1)} collective-permute-done((f32[3,32,512]{2,1,0:T(8,128)S(1)}, f32[3,32,512]{2,1,0:T(8,128)S(1)}, u32[]{:S(2)}, u32[]{:S(2)}) %collective-permute-start.28) | collective-permute-done | bytes 196640 | tf_op jit(solution)/shard_map/ppermute | solution.py:31
  402.2 235.3 %while.35 = (s32[]{:T(128)}, f32[3,8,128]{2,1,0:T(8,128)S(1)}, s32[]{:T(128)}, pred[]{:T(512)}, pred[]{:T(512)}, /*index=5*/f32[16,128]{1,0:T(8,128)S(1)}, f32[3,8,128]{2,1,0:T(8,128)S(1)}, s32[]{:T(128)}, f32[3]{0:T(128)S(1)}) while((s32[]{:T(128)}, f32[3,8,128]{2,1,0:T(8,128)S(1)}, s32[]{:T(128)}, pred[]{:T(512)}, pred[]{:T(512)}, ...), condition=%wide.region_9.10_spmd.clone, body=%wide.region_8.9_spmd.clone.sunk | while | flops 82947 | bytes 585965 | solution.py:117
  410.7 7.3 %collective-permute-done.5 = f32[3,8,128]{2,1,0:T(8,128)S(1)} collective-permute-done((f32[3,8,128]{2,1,0:T(8,128)S(1)}, f32[3,8,128]{2,1,0:T(8,128)S(1)}, u32[]{:S(2)}, u32[]{:S(2)}) %collective-permute-start.5) | collective-permute-done | bytes 12320 | tf_op jit(solution)/shard_map/while/body/eval_jaxpr/ppermute | solution.py:31
  426.3 7.3 %collective-permute-done.5 = f32[3,8,128]{2,1,0:T(8,128)S(1)} collective-permute-done((f32[3,8,128]{2,1,0:T(8,128)S(1)}, f32[3,8,128]{2,1,0:T(8,128)S(1)}, u32[]{:S(2)}, u32[]{:S(2)}) %collective-permute-start.5) | collective-permute-done | bytes 12320 | tf_op jit(solution)/shard_map/while/body/eval_jaxpr/ppermute | solution.py:31
  442.0 7.3 %collective-permute-done.5 = f32[3,8,128]{2,1,0:T(8,128)S(1)} collective-permute-done((f32[3,8,128]{2,1,0:T(8,128)S(1)}, f32[3,8,128]{2,1,0:T(8,128)S(1)}, u32[]{:S(2)}, u32[]{:S(2)}) %collective-permute-start.5) | collective-permute-done | bytes 12320 | tf_op jit(solution)/shard_map/while/body/eval_jaxpr/ppermute | solution.py:31
  457.7 7.3 %collective-permute-done.5 = f32[3,8,128]{2,1,0:T(8,128)S(1)} collective-permute-done((f32[3,8,128]{2,1,0:T(8,128)S(1)}, f32[3,8,128]{2,1,0:T(8,128)S(1)}, u32[]{:S(2)}, u32[]{:S(2)}) %collective-permute-start.5) | collective-permute-done | bytes 12320 | tf_op jit(solution)/shard_map/while/body/eval_jaxpr/ppermute | solution.py:31
  473.4 7.3 %collective-permute-done.5 = f32[3,8,128]{2,1,0:T(8,128)S(1)} collective-permute-done((f32[3,8,128]{2,1,0:T(8,128)S(1)}, f32[3,8,128]{2,1,0:T(8,128)S(1)}, u32[]{:S(2)}, u32[]{:S(2)}) %collective-permute-start.5) | collective-permute-done | bytes 12320 | tf_op jit(solution)/shard_map/while/body/eval_jaxpr/ppermute | solution.py:31
  536.1 7.3 %collective-permute-done.5 = f32[3,8,128]{2,1,0:T(8,128)S(1)} collective-permute-done((f32[3,8,128]{2,1,0:T(8,128)S(1)}, f32[3,8,128]{2,1,0:T(8,128)S(1)}, u32[]{:S(2)}, u32[]{:S(2)}) %collective-permute-start.5) | collective-permute-done | bytes 12320 | tf_op jit(solution)/shard_map/while/body/eval_jaxpr/ppermute | solution.py:31
  (1128 shorter events, 478.3 us)
Async XLA Ops:
  12.1 16.2 %collective-permute-start.24 = (f32[3,4,128]{2,1,0:T(4,128)S(1)}, f32[3,4,128]{2,1,0:T(4,128)S(1)}, u32[]{:S(2)}, u32[]{:S(2)}) collective-permute-start(f32[3,4,128]{2,1,0:T(4,128)S(1)} %get-tuple-element.793), channel_id=1, source_target_pairs={{0,1},{1,2},{2,3},{3,4},{4,5},{5,6},{6,7},{7,8},{8,9},{9,10},{10,1... | collective-permute-start | bytes 18440 | tf_op jit(solution)/shard_map/ppermute | solution.py:22
  12.2 16.2 %collective-permute-start.25 = (f32[3,4,128]{2,1,0:T(4,128)S(1)}, f32[3,4,128]{2,1,0:T(4,128)S(1)}, u32[]{:S(2)}, u32[]{:S(2)}) collective-permute-start(f32[3,4,128]{2,1,0:T(4,128)S(1)} %get-tuple-element.794), channel_id=1, source_target_pairs={{1,0},{2,1},{3,2},{4,3},{5,4},{6,5},{7,6},{8,7},{9,8},{10,9},{11,1... | collective-permute-start | bytes 18440 | tf_op jit(solution)/shard_map/ppermute | solution.py:23
  18.5 9.7 %collective-permute-start.23 = (f32[1,4,128]{2,1,0:T(4,128)S(1)}, f32[1,4,128]{2,1,0:T(4,128)S(1)}, u32[]{:S(2)}, u32[]{:S(2)}) collective-permute-start(f32[1,4,128]{2,1,0:T(4,128)S(1)} %get-tuple-element.849), channel_id=1, source_target_pairs={{1,0},{2,1},{3,2},{4,3},{5,4},{6,5},{7,6},{8,7},{9,8},{10,9},{11,1... | collective-permute-start | bytes 6152 | tf_op jit(solution)/shard_map/ppermute | solution.py:23
  92.8 9.4 %collective-permute-start.2 = (f32[3,8,128]{2,1,0:T(8,128)S(1)}, f32[3,8,128]{2,1,0:T(8,128)S(1)}, u32[]{:S(2)}, u32[]{:S(2)}) collective-permute-start(f32[3,8,128]{2,1,0:T(8,128)S(1)} %maximum_add_fusion.8), channel_id=1, source_target_pairs={{0,16},{16,32},{32,48},{48,64},{64,80},{80,96},{96,112},{112,128},... | collective-permute-start | bytes 36872 | tf_op jit(solution)/shard_map/while/body/eval_jaxpr/ppermute | solution.py:31
  108.7 9.2 %collective-permute-start.2 = (f32[3,8,128]{2,1,0:T(8,128)S(1)}, f32[3,8,128]{2,1,0:T(8,128)S(1)}, u32[]{:S(2)}, u32[]{:S(2)}) collective-permute-start(f32[3,8,128]{2,1,0:T(8,128)S(1)} %maximum_add_fusion.8), channel_id=1, source_target_pairs={{0,16},{16,32},{32,48},{48,64},{64,80},{80,96},{96,112},{112,128},... | collective-permute-start | bytes 36872 | tf_op jit(solution)/shard_map/while/body/eval_jaxpr/ppermute | solution.py:31
  124.3 9.2 %collective-permute-start.2 = (f32[3,8,128]{2,1,0:T(8,128)S(1)}, f32[3,8,128]{2,1,0:T(8,128)S(1)}, u32[]{:S(2)}, u32[]{:S(2)}) collective-permute-start(f32[3,8,128]{2,1,0:T(8,128)S(1)} %maximum_add_fusion.8), channel_id=1, source_target_pairs={{0,16},{16,32},{32,48},{48,64},{64,80},{80,96},{96,112},{112,128},... | collective-permute-start | bytes 36872 | tf_op jit(solution)/shard_map/while/body/eval_jaxpr/ppermute | solution.py:31
  140.0 9.2 %collective-permute-start.2 = (f32[3,8,128]{2,1,0:T(8,128)S(1)}, f32[3,8,128]{2,1,0:T(8,128)S(1)}, u32[]{:S(2)}, u32[]{:S(2)}) collective-permute-start(f32[3,8,128]{2,1,0:T(8,128)S(1)} %maximum_add_fusion.8), channel_id=1, source_target_pairs={{0,16},{16,32},{32,48},{48,64},{64,80},{80,96},{96,112},{112,128},... | collective-permute-start | bytes 36872 | tf_op jit(solution)/shard_map/while/body/eval_jaxpr/ppermute | solution.py:31
  155.7 9.2 %collective-permute-start.2 = (f32[3,8,128]{2,1,0:T(8,128)S(1)}, f32[3,8,128]{2,1,0:T(8,128)S(1)}, u32[]{:S(2)}, u32[]{:S(2)}) collective-permute-start(f32[3,8,128]{2,1,0:T(8,128)S(1)} %maximum_add_fusion.8), channel_id=1, source_target_pairs={{0,16},{16,32},{32,48},{48,64},{64,80},{80,96},{96,112},{112,128},... | collective-permute-start | bytes 36872 | tf_op jit(solution)/shard_map/while/body/eval_jaxpr/ppermute | solution.py:31
  171.4 9.2 %collective-permute-start.2 = (f32[3,8,128]{2,1,0:T(8,128)S(1)}, f32[3,8,128]{2,1,0:T(8,128)S(1)}, u32[]{:S(2)}, u32[]{:S(2)}) collective-permute-start(f32[3,8,128]{2,1,0:T(8,128)S(1)} %maximum_add_fusion.8), channel_id=1, source_target_pairs={{0,16},{16,32},{32,48},{48,64},{64,80},{80,96},{96,112},{112,128},... | collective-permute-start | bytes 36872 | tf_op jit(solution)/shard_map/while/body/eval_jaxpr/ppermute | solution.py:31
  187.1 9.2 %collective-permute-start.2 = (f32[3,8,128]{2,1,0:T(8,128)S(1)}, f32[3,8,128]{2,1,0:T(8,128)S(1)}, u32[]{:S(2)}, u32[]{:S(2)}) collective-permute-start(f32[3,8,128]{2,1,0:T(8,128)S(1)} %maximum_add_fusion.8), channel_id=1, source_target_pairs={{0,16},{16,32},{32,48},{48,64},{64,80},{80,96},{96,112},{112,128},... | collective-permute-start | bytes 36872 | tf_op jit(solution)/shard_map/while/body/eval_jaxpr/ppermute | solution.py:31
  202.8 9.2 %collective-permute-start.2 = (f32[3,8,128]{2,1,0:T(8,128)S(1)}, f32[3,8,128]{2,1,0:T(8,128)S(1)}, u32[]{:S(2)}, u32[]{:S(2)}) collective-permute-start(f32[3,8,128]{2,1,0:T(8,128)S(1)} %maximum_add_fusion.8), channel_id=1, source_target_pairs={{0,16},{16,32},{32,48},{48,64},{64,80},{80,96},{96,112},{112,128},... | collective-permute-start | bytes 36872 | tf_op jit(solution)/shard_map/while/body/eval_jaxpr/ppermute | solution.py:31
  218.5 9.2 %collective-permute-start.2 = (f32[3,8,128]{2,1,0:T(8,128)S(1)}, f32[3,8,128]{2,1,0:T(8,128)S(1)}, u32[]{:S(2)}, u32[]{:S(2)}) collective-permute-start(f32[3,8,128]{2,1,0:T(8,128)S(1)} %maximum_add_fusion.8), channel_id=1, source_target_pairs={{0,16},{16,32},{32,48},{48,64},{64,80},{80,96},{96,112},{112,128},... | collective-permute-start | bytes 36872 | tf_op jit(solution)/shard_map/while/body/eval_jaxpr/ppermute | solution.py:31
  234.1 9.2 %collective-permute-start.2 = (f32[3,8,128]{2,1,0:T(8,128)S(1)}, f32[3,8,128]{2,1,0:T(8,128)S(1)}, u32[]{:S(2)}, u32[]{:S(2)}) collective-permute-start(f32[3,8,128]{2,1,0:T(8,128)S(1)} %maximum_add_fusion.8), channel_id=1, source_target_pairs={{0,16},{16,32},{32,48},{48,64},{64,80},{80,96},{96,112},{112,128},... | collective-permute-start | bytes 36872 | tf_op jit(solution)/shard_map/while/body/eval_jaxpr/ppermute | solution.py:31
  249.8 9.2 %collective-permute-start.2 = (f32[3,8,128]{2,1,0:T(8,128)S(1)}, f32[3,8,128]{2,1,0:T(8,128)S(1)}, u32[]{:S(2)}, u32[]{:S(2)}) collective-permute-start(f32[3,8,128]{2,1,0:T(8,128)S(1)} %maximum_add_fusion.8), channel_id=1, source_target_pairs={{0,16},{16,32},{32,48},{48,64},{64,80},{80,96},{96,112},{112,128},... | collective-permute-start | bytes 36872 | tf_op jit(solution)/shard_map/while/body/eval_jaxpr/ppermute | solution.py:31
  265.5 9.2 %collective-permute-start.2 = (f32[3,8,128]{2,1,0:T(8,128)S(1)}, f32[3,8,128]{2,1,0:T(8,128)S(1)}, u32[]{:S(2)}, u32[]{:S(2)}) collective-permute-start(f32[3,8,128]{2,1,0:T(8,128)S(1)} %maximum_add_fusion.8), channel_id=1, source_target_pairs={{0,16},{16,32},{32,48},{48,64},{64,80},{80,96},{96,112},{112,128},... | collective-permute-start | bytes 36872 | tf_op jit(solution)/shard_map/while/body/eval_jaxpr/ppermute | solution.py:31
  281.2 9.2 %collective-permute-start.2 = (f32[3,8,128]{2,1,0:T(8,128)S(1)}, f32[3,8,128]{2,1,0:T(8,128)S(1)}, u32[]{:S(2)}, u32[]{:S(2)}) collective-permute-start(f32[3,8,128]{2,1,0:T(8,128)S(1)} %maximum_add_fusion.8), channel_id=1, source_target_pairs={{0,16},{16,32},{32,48},{48,64},{64,80},{80,96},{96,112},{112,128},... | collective-permute-start | bytes 36872 | tf_op jit(solution)/shard_map/while/body/eval_jaxpr/ppermute | solution.py:31
  296.9 9.2 %collective-permute-start.2 = (f32[3,8,128]{2,1,0:T(8,128)S(1)}, f32[3,8,128]{2,1,0:T(8,128)S(1)}, u32[]{:S(2)}, u32[]{:S(2)}) collective-permute-start(f32[3,8,128]{2,1,0:T(8,128)S(1)} %maximum_add_fusion.8), channel_id=1, source_target_pairs={{0,16},{16,32},{32,48},{48,64},{64,80},{80,96},{96,112},{112,128},... | collective-permute-start | bytes 36872 | tf_op jit(solution)/shard_map/while/body/eval_jaxpr/ppermute | solution.py:31
  312.6 9.2 %collective-permute-start.2 = (f32[3,8,128]{2,1,0:T(8,128)S(1)}, f32[3,8,128]{2,1,0:T(8,128)S(1)}, u32[]{:S(2)}, u32[]{:S(2)}) collective-permute-start(f32[3,8,128]{2,1,0:T(8,128)S(1)} %maximum_add_fusion.8), channel_id=1, source_target_pairs={{0,16},{16,32},{32,48},{48,64},{64,80},{80,96},{96,112},{112,128},... | collective-permute-start | bytes 36872 | tf_op jit(solution)/shard_map/while/body/eval_jaxpr/ppermute | solution.py:31
  328.8 11.2 %collective-permute-start.28 = (f32[3,32,512]{2,1,0:T(8,128)S(1)}, f32[3,32,512]{2,1,0:T(8,128)S(1)}, u32[]{:S(2)}, u32[]{:S(2)}) collective-permute-start(f32[3,32,512]{2,1,0:T(8,128)S(1)} %maximum_add_fusion.2), channel_id=1, source_target_pairs={{0,16},{16,32},{32,48},{48,64},{64,80},{80,96},{96,112},{112,128},... | collective-permute-start | bytes 589832 | tf_op jit(solution)/shard_map/ppermute | solution.py:31
  408.7 9.2 %collective-permute-start.5 = (f32[3,8,128]{2,1,0:T(8,128)S(1)}, f32[3,8,128]{2,1,0:T(8,128)S(1)}, u32[]{:S(2)}, u32[]{:S(2)}) collective-permute-start(f32[3,8,128]{2,1,0:T(8,128)S(1)} %maximum_add_fusion.9), channel_id=1, source_target_pairs={{0,16},{16,32},{32,48},{48,64},{64,80},{80,96},{96,112},{112,128},... | collective-permute-start | bytes 36872 | tf_op jit(solution)/shard_map/while/body/eval_jaxpr/ppermute | solution.py:31
  487.1 9.2 %collective-permute-start.5 = (f32[3,8,128]{2,1,0:T(8,128)S(1)}, f32[3,8,128]{2,1,0:T(8,128)S(1)}, u32[]{:S(2)}, u32[]{:S(2)}) collective-permute-start(f32[3,8,128]{2,1,0:T(8,128)S(1)} %maximum_add_fusion.9), channel_id=1, source_target_pairs={{0,16},{16,32},{32,48},{48,64},{64,80},{80,96},{96,112},{112,128},... | collective-permute-start | bytes 36872 | tf_op jit(solution)/shard_map/while/body/eval_jaxpr/ppermute | solution.py:31
  502.8 9.2 %collective-permute-start.5 = (f32[3,8,128]{2,1,0:T(8,128)S(1)}, f32[3,8,128]{2,1,0:T(8,128)S(1)}, u32[]{:S(2)}, u32[]{:S(2)}) collective-permute-start(f32[3,8,128]{2,1,0:T(8,128)S(1)} %maximum_add_fusion.9), channel_id=1, source_target_pairs={{0,16},{16,32},{32,48},{48,64},{64,80},{80,96},{96,112},{112,128},... | collective-permute-start | bytes 36872 | tf_op jit(solution)/shard_map/while/body/eval_jaxpr/ppermute | solution.py:31
  518.5 9.2 %collective-permute-start.5 = (f32[3,8,128]{2,1,0:T(8,128)S(1)}, f32[3,8,128]{2,1,0:T(8,128)S(1)}, u32[]{:S(2)}, u32[]{:S(2)}) collective-permute-start(f32[3,8,128]{2,1,0:T(8,128)S(1)} %maximum_add_fusion.9), channel_id=1, source_target_pairs={{0,16},{16,32},{32,48},{48,64},{64,80},{80,96},{96,112},{112,128},... | collective-permute-start | bytes 36872 | tf_op jit(solution)/shard_map/while/body/eval_jaxpr/ppermute | solution.py:31
  534.2 9.2 %collective-permute-start.5 = (f32[3,8,128]{2,1,0:T(8,128)S(1)}, f32[3,8,128]{2,1,0:T(8,128)S(1)}, u32[]{:S(2)}, u32[]{:S(2)}) collective-permute-start(f32[3,8,128]{2,1,0:T(8,128)S(1)} %maximum_add_fusion.9), channel_id=1, source_target_pairs={{0,16},{16,32},{32,48},{48,64},{64,80},{80,96},{96,112},{112,128},... | collective-permute-start | bytes 36872 | tf_op jit(solution)/shard_map/while/body/eval_jaxpr/ppermute | solution.py:31
  (115 other events, 676.7 us)
where the time goes:
time: 657 us; the launch traced here: 645 us
  waiting for transfers between devices  287 us (44%)
  starting transfers between devices  258 us (39%)
  local copies, waits for them, and re-layouts  71.8 us (11%)
  other arithmetic  24.3 us (4%)
    ppermute x31, waiting for transfers between devices, passed_along(): return lax.ppermute(block, axis, route)  225 us
    ppermute x50, starting transfers between devices, with_halo(): after = lax.ppermute(initial, axis, down)  193 us
    ppermute x50, waiting for transfers between devices, with_halo(): before = lax.ppermute(last, axis, up)  61.5 us
    ppermute x31, starting transfers between devices, passed_along(): return lax.ppermute(block, axis, route)  61.3 us
    rev x100, local copies, waits for them, and re-layouts, reflect(): return jnp.where(flag, field_signs * jnp.flip(rim, -1), rim)  18.4 us
    another operation x12, local copies, waits for them, and re-layouts, advance(): return jnp.stack([height_core, across_new, along_new])  16.7 us
  transfers between devices with their start and end apart: 131, of which 80 were waited for; matrix products, arithmetic and copies ran while one was open for 2% of the time, Pallas kernels for 0%

commit v1 on v0

v1 whole, which is shorter than its diff:
```python
import jax
import jax.numpy as jnp
from jax import lax
from jax.experimental import pallas as pl
from jax.experimental.pallas import tpu as pltpu
from jax.sharding import PartitionSpec as P

MESH = pl.DeviceIdType.MESH
NT = 16
NK = 16
HC = 0.45
FC = 24
FR = 88
CC = 80
CR = 168
ROUND_A = ((3, 2), (2, 1), (1, 1))
ROUND_B = ((12, 6), (8, 4), (4, 2))


def gather(x, idx):
    return jnp.take_along_axis(x, idx, axis=1)


def ahead(x):
    return pltpu.roll(x, 127, 1)


def behind(x):
    return pltpu.roll(x, 1, 1)


def coarse_step(st, e_ref, q, first, blocks):
    for b in range(blocks + 1):
        r = first - 1 + 8 * b
        g = st[0, pl.ds(r, 8), :] - HC * (st[1, pl.ds(r + 1, 8), :] - st[1, pl.ds(r - 1, 8), :])
        v = st[2, pl.ds(r, 8), :]
        wide = pltpu.roll(v, 126, 1) - 2.0 * v + pltpu.roll(v, 2, 1)
        st[0, pl.ds(r, 8), :] = g - HC * (ahead(v) - behind(v))
        e_ref[pl.ds(r, 8), :] = HC * ((ahead(g) - behind(g)) - HC * wide)
    for b in range(blocks):
        r = first + 8 * b
        u, v, rate = st[1, pl.ds(r, 8), :], st[2, pl.ds(r, 8), :], q[pl.ds(r, 8), :]
        new = u + rate * v - HC * (st[0, pl.ds(r + 1, 8), :] - st[0, pl.ds(r - 1, 8), :])
        st[1, pl.ds(r, 8), :] = new
        st[2, pl.ds(r, 8), :] = v - rate * new - e_ref[pl.ds(r, 8), :]


def coarse(st, e_ref, q, first, rows):
    coarse_step(st, e_ref, q, first - 2, rows // 8 + 1)
    coarse_step(st, e_ref, q, first, rows // 8)


def fine_step(st, e_ref, q, first, blocks):
    for b in range(blocks + 1):
        r = first - 1 + 8 * b
        v = [st[2, c, pl.ds(r, 8), :] for c in range(4)]
        g = [
            st[0, c, pl.ds(r, 8), :] - HC * (st[1, c, pl.ds(r + 1, 8), :] - st[1, c, pl.ds(r - 1, 8), :])
            for c in range(4)
        ]
        vs = [behind(v[2]), behind(v[3])] + v + [ahead(v[0]), ahead(v[1])]
        gs = [behind(g[3])] + g + [ahead(g[0])]
        for c in range(4):
            st[0, c, pl.ds(r, 8), :] = g[c] - HC * (vs[c + 3] - vs[c + 1])
            e_ref[c, pl.ds(r, 8), :] = HC * ((gs[c + 2] - gs[c]) - HC * (vs[c + 4] - 2.0 * v[c] + vs[c]))
    for b in range(blocks):
        r = first + 8 * b
        for c in range(4):
            u, v, rate = st[1, c, pl.ds(r, 8), :], st[2, c, pl.ds(r, 8), :], q[c, pl.ds(r, 8), :]
            new = u + rate * v - HC * (st[0, c, pl.ds(r + 1, 8), :] - st[0, c, pl.ds(r - 1, 8), :])
            st[1, c, pl.ds(r, 8), :] = new
            st[2, c, pl.ds(r, 8), :] = v - rate * new - e_ref[c, pl.ds(r, 8), :]


def fine_run(st, e_ref, q):
    for first, blocks in ((0, 8), (2, 7), (4, 6), (6, 5)):
        def one(s, carry, first=first, blocks=blocks):
            fine_step(st, e_ref, q, 10 + 2 * (first + s), blocks)
            return carry

        lax.fori_loop(0, 2, one, 0)


def restrict(ref, first):
    total = None
    for j in range(4):
        for c in range(4):
            part = ref[c, pl.ds(first + j, 8, stride=4), :]
            total = part if total is None else total + part
    return total


def kernel(initial, rotation, flips, out, xin, rin, own, own_q, halo, halo_q, fine, fine_q, fine_e, first_run, halo_f,
           rates, rate_own, rate_ring, start_own, start_ring, ring, ring_e, total, anchor_old, work, term_own, term_in,
           part_own, part_in, fine_out, load_sem, send_sem, halo_sem, ring_sem, a_sem, b_sem):
    k = lax.axis_index("tm")
    t = lax.axis_index("tile")
    lane = lax.broadcasted_iota(jnp.int32, (8, 128), 1)
    turned = 127 - lane

    def tile_at(o):
        return lax.rem(t + (o + NT), NT)

    load_x = pltpu.make_async_copy(initial, xin, load_sem.at[0])
    load_q = pltpu.make_async_copy(rotation, rin, load_sem.at[1])
    load_x.start()
    load_q.start()

    barrier = pltpu.get_barrier_semaphore()
    for o in range(1, NT):
        pl.semaphore_signal(barrier, inc=1, device_id=(k, tile_at(o)), device_id_type=MESH)
    expected = NT - 1
    for distance, reach in ROUND_A + ROUND_B:
        @pl.when(k >= distance)
        def _(distance=distance, reach=reach):
            for o in range(-reach, reach + 1):
                pl.semaphore_signal(barrier, inc=1, device_id=(k - distance, tile_at(o)), device_id_type=MESH)

        expected = expected + jnp.where(k + distance < NK, 2 * reach + 1, 0)

    odd = {0: None}
    up = down = jnp.int32(0)
    for o in range(1, NT // 2 + 1):
        up = up + jnp.where(flips[tile_at(o)] != 0, 1, 0)
        down = down + jnp.where(flips[tile_at(1 - o)] != 0, 1, 0)
        odd[o] = (jnp.zeros((8, 128), jnp.int32) + lax.rem(up, 2)) != 0
        odd[-o] = (jnp.zeros((8, 128), jnp.int32) + lax.rem(down, 2)) != 0

    def turn(x, o, negate, other=None):
        if o == 0:
            return x
        back = gather(x if other is None else other, turned)
        return jnp.where(odd[o], -back if negate else back, x)

    def oriented(src, o):
        return [turn(src[f], o, f == 2) for f in range(3)]

    zero = jnp.zeros((8, 128), jnp.float32)
    for f in range(3):
        for b in range(CR // 8):
            work[f, 8 * b : 8 * b + 8, :] = zero
        for b in (0, 1, CR // 8 - 2, CR // 8 - 1):
            ring[f, 8 * b : 8 * b + 8, :] = zero
        for c in range(4):
            for b in (0, FR // 8 - 2, FR // 8 - 1):
                fine[f, c, 8 * b : 8 * b + 8, :] = zero
        total[f] = jnp.zeros((16, 128), jnp.float32)
    for b in (0, 1, CR // 8 - 2, CR // 8 - 1):
        rates[8 * b : 8 * b + 8, :] = zero
    for c in range(4):
        for b in (0, FR // 8 - 2, FR // 8 - 1):
            fine_q[c, 8 * b : 8 * b + 8, :] = zero

    quarter = lane // 32
    apart = 4 * lax.rem(lane, 32)

    def spread(load, store):
        x = [load(s) for s in range(4)]
        for c in range(4):
            y = [gather(x[s], apart + c) for s in range(4)]
            store(c, jnp.where(quarter < 2, jnp.where(quarter == 0, y[0], y[1]), jnp.where(quarter == 2, y[2], y[3])))

    load_q.wait()
    for b in range(4):
        def store_q(c, x, b=b):
            own_q[c, 8 * b : 8 * b + 8, :] = x
            fine_q[c, FC + 8 * b : FC + 8 * b + 8, :] = x

        spread(lambda s, b=b: rin[8 * b : 8 * b + 8, 128 * s : 128 * s + 128], store_q)
    load_x.wait()
    for f in range(3):
        for b in range(4):
            def store_x(c, x, f=f, b=b):
                own[f, c, 8 * b : 8 * b + 8, :] = x
                fine[f, c, FC + 8 * b : FC + 8 * b + 8, :] = x

            spread(lambda s, f=f, b=b: xin[f, 8 * b : 8 * b + 8, 128 * s : 128 * s + 128], store_x)

    pl.semaphore_wait(barrier, expected)

    def send(src, dst, recv, where):
        pltpu.make_async_remote_copy(
            src_ref=src, dst_ref=dst, send_sem=send_sem, recv_sem=recv, device_id=where, device_id_type=MESH
        ).start()

    def take(ref, sem):
        pltpu.make_async_copy(ref, ref, sem).wait()

    send(own.at[:, :, pl.ds(16, 16), :], halo.at[0], halo_sem.at[0], (k, tile_at(1)))
    send(own.at[:, :, pl.ds(0, 16), :], halo.at[1], halo_sem.at[1], (k, tile_at(-1)))
    send(own_q.at[:, pl.ds(16, 16), :], halo_q.at[0], halo_sem.at[2], (k, tile_at(1)))
    send(own_q.at[:, pl.ds(0, 16), :], halo_q.at[1], halo_sem.at[3], (k, tile_at(-1)))
    rate_own[...] = restrict(own_q, 0) * 0.25
    for o in range(1, NT):
        send(rate_own, rate_ring.at[NT - o - 1], ring_sem.at[0], (k, tile_at(o)))

    take(halo_q.at[0], halo_sem.at[2])
    take(halo_q.at[1], halo_sem.at[3])
    for side, o, row in ((0, -1, FC - 16), (1, 1, FC + 32)):
        for b in range(2):
            for c in range(4):
                x, y = (halo_q[side, cc, 8 * b : 8 * b + 8, :] for cc in (c, 3 - c))
                fine_q[c, row + 8 * b : row + 8 * b + 8, :] = turn(x, o, True, y)

    def fill_rims(src, sem):
        for side, o, row in ((0, -1, FC - 16), (1, 1, FC + 32)):
            take(src.at[side], sem.at[side])
            for f in range(3):
                for b in range(2):
                    for c in range(4):
                        x, y = (src[side, f, cc, 8 * b : 8 * b + 8, :] for cc in (c, 3 - c))
                        fine[f, c, row + 8 * b : row + 8 * b + 8, :] = turn(x, o, f == 2, y)

    fill_rims(halo, halo_sem)
    for f in range(3):
        for half in range(2):
            work[f, pl.ds(CC - 4 + 8 * half, 8), :] = restrict(fine.at[f], FC - 16 + 32 * half) * 0.0625
        anchor_old[f] = work[f, pl.ds(CC, 8), :]
    fine_run(fine, fine_e, fine_q)
    for f in range(3):
        start = restrict(fine.at[f], FC) * 0.0625 - anchor_old[f]
        start_own[f] = start
        ring[f, CC : CC + 8, :] = start
    for o in range(1, NT):
        send(start_own, start_ring.at[NT - o - 1], ring_sem.at[1], (k, tile_at(o)))
    for f in range(3):
        for c in range(4):
            first_run[f, c] = fine[f, c, FC : FC + 32, :]
    send(first_run.at[:, :, pl.ds(16, 16), :], halo_f.at[0], halo_sem.at[4], (k, tile_at(1)))
    send(first_run.at[:, :, pl.ds(0, 16), :], halo_f.at[1], halo_sem.at[5], (k, tile_at(-1)))

    offsets = [o for o in range(-(NT // 2), NT // 2 + 1) if o]
    take(rate_ring, ring_sem.at[0])
    rates[CC : CC + 8, :] = rate_own[...]
    for o in offsets:
        rates[CC + 8 * o : CC + 8 * o + 8, :] = turn(rate_ring[(o + NT) % NT - 1], o, True)
    coarse(work, ring_e, rates, CC, 8)
    for f in range(3):
        anchor_old[f] = work[f, CC : CC + 8, :]

    take(start_ring, ring_sem.at[1])
    for o in offsets:
        for f, x in enumerate(oriented(start_ring.at[(o + NT) % NT - 1], o)):
            ring[f, CC + 8 * o : CC + 8 * o + 8, :] = x

    for m in (3, 2, 1, 0):
        def chain(s, carry, m=m):
            coarse(ring, ring_e, rates, CC - 16 - 16 * m, 40 + 32 * m)
            for f in range(3):
                total[f] = total[f] + ring[f, pl.ds(CC - 4, 16), :]
            return carry

        lax.fori_loop(0, jnp.clip(k - 1 - 4 * m, 0, 4), chain, 0)

    fill_rims(halo_f, halo_sem.at[pl.ds(4, 2)])
    for f in range(3):
        more = total[f]
        for c in range(4):
            for j in range(4):
                rows = pl.ds(FC - 16 + j, 16, stride=4)
                fine[f, c, rows, :] = fine[f, c, rows, :] + more
    coarse(ring, ring_e, rates, CC, 8)
    for f in range(3):
        anchor_old[f] = anchor_old[f] + total[f, pl.ds(4, 8), :] + ring[f, CC : CC + 8, :]
    fine_run(fine, fine_e, fine_q)

    @pl.when(k == 0)
    def _():
        for f in range(3):
            anchor_old[f] = zero
            for c in range(4):
                fine[f, c, FC : FC + 32, :] = first_run[f, c]

    for f in range(3):
        mean = restrict(fine.at[f], FC) * 0.0625
        start_own_f = mean - anchor_old[f]
        total[f, 0:8, :] = mean
        term_own[f] = start_own_f

    def places(stages):
        at, base = {}, 0
        for distance, reach in stages:
            at[distance] = base
            base += 2 * reach + 1
        return at

    def prefix(stages, src, landing, sems, applications):
        at = places(stages)
        for stage, (distance, reach) in reversed(list(enumerate(stages))):
            @pl.when(k + distance < NK)
            def _(stage=stage, distance=distance, reach=reach):
                for o in range(-reach, reach + 1):
                    send(src, landing.at[at[distance] + reach - o], sems.at[stage], (k + distance, tile_at(o)))

        for stage, (distance, reach) in enumerate(stages):
            @pl.when(k >= distance)
            def _(stage=stage, distance=distance, reach=reach):
                base = at[distance]
                take(landing.at[pl.ds(base, 2 * reach + 1)], sems.at[stage])
                for o in range(-reach, reach + 1):
                    for f, x in enumerate(oriented(landing.at[base + reach + o], o)):
                        rows = slice(CC + 8 * o, CC + 8 * o + 8)
                        work[f, rows, :] = work[f, rows, :] + x
                if applications == 1:
                    coarse(work, ring_e, rates, CC - 4 * (distance - 1), 8 * distance)
                else:
                    def apply(s, carry):
                        coarse(work, ring_e, rates, CC - 4 * (distance - 1), 8 * distance)
                        return carry

                    lax.fori_loop(0, applications, apply, 0)

    def clear():
        for f in range(3):
            for b in range(CR // 8):
                work[f, 8 * b : 8 * b + 8, :] = zero

    clear()
    prefix(ROUND_A, term_own, term_in, a_sem, 1)
    for f in range(3):
        part_own[f] = work[f, CC : CC + 8, :] + term_own[f]
    clear()
    prefix(ROUND_B, part_own, part_in, b_sem, 4)

    apart_out = lane // 4
    phase = lax.rem(lane, 4)
    for f in range(3):
        extra = work[f, CC : CC + 8, :] + part_own[f] - total[f, 0:8, :]
        for c in range(4):
            for j in range(4):
                rows = pl.ds(FC + j, 8, stride=4)
                fine[f, c, rows, :] = fine[f, c, rows, :] + extra
        for b in range(4):
            z = [fine[f, c, FC + 8 * b : FC + 8 * b + 8, :] for c in range(4)]
            for s in range(4):
                y = [gather(z[c], apart_out + 32 * s) for c in range(4)]
                out[0, f, 8 * b : 8 * b + 8, 128 * s : 128 * s + 128] = jnp.where(
                    phase < 2, jnp.where(phase == 0, y[0], y[1]), jnp.where(phase == 2, y[2], y[3])
                )

    for _ in range(2):
        take(halo, send_sem)
    take(halo_q, send_sem)
    take(rate_ring, send_sem)
    take(start_ring, send_sem)
    for stages, landing in ((ROUND_A, term_in), (ROUND_B, part_in)):
        at = places(stages)
        for distance, reach in stages:
            @pl.when(k + distance < NK)
            def _(landing=landing, base=at[distance], count=2 * reach + 1):
                take(landing.at[pl.ds(base, count)], send_sem)


def body(initial, rotation, seam_flip):
    def vmem(*shape):
        return pltpu.VMEM(shape, jnp.float32)

    dma = pltpu.SemaphoreType.DMA
    scratch = [
        vmem(3, 32, 512), vmem(32, 512),
        vmem(3, 4, 32, 128), vmem(4, 32, 128),
        vmem(2, 3, 4, 16, 128), vmem(2, 4, 16, 128),
        vmem(3, 4, FR, 128), vmem(4, FR, 128), vmem(4, FR, 128),
        vmem(3, 4, 32, 128), vmem(2, 3, 4, 16, 128),
        vmem(CR, 128), vmem(8, 128), vmem(NT - 1, 8, 128),
        vmem(3, 8, 128), vmem(NT - 1, 3, 8, 128),
        vmem(3, CR, 128), vmem(CR, 128),
        vmem(3, 16, 128), vmem(3, 8, 128),
        vmem(3, CR, 128),
        vmem(3, 8, 128), vmem(11, 3, 8, 128),
        vmem(3, 8, 128), vmem(27, 3, 8, 128),
        vmem(8, 128),
        dma((2,)), dma, dma((6,)), dma((2,)), dma((3,)), dma((3,)),
    ]
    return pl.pallas_call(
        kernel,
        out_shape=jax.ShapeDtypeStruct((1, 3, 32, 512), jnp.float32),
        in_specs=[
            pl.BlockSpec(memory_space=pl.ANY),
            pl.BlockSpec(memory_space=pl.ANY),
            pl.BlockSpec(memory_space=pltpu.SMEM),
        ],
        out_specs=pl.BlockSpec(memory_space=pltpu.VMEM),
        scratch_shapes=scratch,
        compiler_params=pltpu.CompilerParams(
            collective_id=0, has_side_effects=True, vmem_limit_bytes=24 * 1024 * 1024
        ),
        name="parareal",
    )(initial, rotation, seam_flip)


def solution(mesh):
    in_specs = (P(None, "tile", None), P("tile", None), P())
    out_specs = P("tm", None, "tile", None)
    return jax.shard_map(body, mesh=mesh, in_specs=in_specs, out_specs=out_specs, check_vma=False)
```

time: 657 us -> 53.1 us (0.08); the launches traced: 645 us -> 52.5 us
  waiting for transfers between devices: 287 us -> 0 us
  starting transfers between devices: 258 us -> 0 us
  local copies, waits for them, and re-layouts: 71.8 us -> 3.1 us
  Pallas kernels: 0 us -> 49.3 us
  other arithmetic: 24.3 us -> 0 us
    ppermute x131 -> x0, waiting for transfers between devices: 287 us -> none  [the longest x31 225 us: passed_along(): return lax.ppermute(block, axis, route)]
    ppermute x131 -> x0, starting transfers between devices: 258 us -> none  [the longest x50 193 us: with_halo(): after = lax.ppermute(initial, axis, down)]
    pallas_call x0 -> x1, Pallas kernels: none -> 49.3 us  [body(): pl.pallas_call(kernel, out_shape=jax.ShapeDtypeStruct((1, 3, 32, 512), jn...]
    slice x397 -> x0, local copies, waits for them, and re-layouts: 24.8 us -> none  [the longest x164 12.2 us: advance(): jnp.roll(height_core, 1, -1)]
    rev x100 -> x0, local copies, waits for them, and re-layouts: 18.4 us -> none  [reflect(): return jnp.where(flag, field_signs * jnp.flip(rim, -1), rim)]
    another operation x12 -> x0, local copies, waits for them, and re-layouts: 16.7 us -> none  [advance(): return jnp.stack([height_core, across_new, along_new])]
    sub x135 -> x0, other arithmetic: 11.6 us -> none  [the longest x82 7.31 us: advance(): height_new = height[..., 1:-1, :] - courant * (across_slope + along_slope)]
    reshape x6 -> x0, local copies, waits for them, and re-layouts: 11.6 us -> none  [the longest x2 10.9 us: restrict(): field_in.reshape(field_shape[:-2] + (field_shape[-2] // FACTOR, FACTOR, f...]
  transfers between devices with their start and end apart: 131 -> 0, of which waited for: 80 -> 0; matrix products, arithmetic and copies ran while one was open for 2% -> 0% of each run, Pallas kernels for 0% -> 0%
where the time goes in v1:
time: 53.1 us; the launch traced here: 52.5 us
  Pallas kernels  49.3 us (93%)
  local copies, waits for them, and re-layouts  3.1 us (6%)
    pallas_call x1, Pallas kernels, body(): pl.pallas_call(kernel, out_shape=jax.ShapeDtypeStruct((1, 3, 32, 512), jn...  49.3 us
    unnamed x7, local copies, waits for them, and re-layouts  3.1 us

profile of v1, /device:TPU:4, one launch (start us, length us, event | category | flops | bytes accessed | tf_op | source)
XLA Modules:
  0.0 52.5 jit_solution(82893972114847695)
XLA Ops:
  0.0 0.0 copy-start
  0.0 0.9 %copy-done = f32[3,32,512]{2,1,0:T(8,128)S(1)} copy-done((f32[3,32,512]{2,1,0:T(8,128)S(1)}, f32[3,32,512]{2,1,0:T(8,128)}, u32[]{:S(2)}) %copy-start) | copy-done | bytes 196632
  0.9 0.0 copy-start.1
  0.9 0.8 %copy-done.1 = f32[32,512]{1,0:T(8,128)S(1)} copy-done((f32[32,512]{1,0:T(8,128)S(1)}, f32[32,512]{1,0:T(8,128)}, u32[]{:S(2)}) %copy-start.1) | copy-done | bytes 65560
  1.8 0.0 copy-start.2
  1.8 0.7 %copy-done.2 = s32[16]{0:T(128)S(1)} copy-done((s32[16]{0:T(128)S(1)}, s32[16]{0:T(128)}, u32[]{:S(2)}) %copy-start.2) | copy-done | bytes 88
  2.4 49.3 %parareal.1 = f32[1,3,32,512]{3,2,1,0:T(8,128)S(1)} custom-call(f32[3,32,512]{2,1,0:T(8,128)S(1)} %copy-done, f32[32,512]{1,0:T(8,128)S(1)} %copy-done.1, s32[16]{0:T(128)S(1)} %copy-done.2), custom_call_target="tpu_custom_call" | custom-call | tf_op jit(solution)/shard_map/parareal/pallas_call | solution.py:375
  51.8 0.7 %copy.5 = f32[1,3,32,512]{3,2,1,0:T(8,128)} copy(f32[1,3,32,512]{3,2,1,0:T(8,128)S(1)} %parareal.1) | data formatting | bytes 393216
Async XLA Ops:
  0.0 0.9 %copy-start = (f32[3,32,512]{2,1,0:T(8,128)S(1)}, f32[3,32,512]{2,1,0:T(8,128)}, u32[]{:S(2)}) copy-start(f32[3,32,512]{2,1,0:T(8,128)} %initial.1) | copy-start | bytes 589828
  0.9 0.8 %copy-start.1 = (f32[32,512]{1,0:T(8,128)S(1)}, f32[32,512]{1,0:T(8,128)}, u32[]{:S(2)}) copy-start(f32[32,512]{1,0:T(8,128)} %rotation.1) | copy-start | bytes 196612
  1.8 0.7 %copy-start.2 = (s32[16]{0:T(128)S(1)}, s32[16]{0:T(128)}, u32[]{:S(2)}) copy-start(s32[16]{0:T(128)} %flips.1) | copy-start | bytes 196

commit v2 on v1

--- a/solution.py
+++ b/solution.py
@@ -13,8 +13,8 @@
 FR = 88
 CC = 80
 CR = 168
-ROUND_A = ((3, 2), (2, 1), (1, 1))
-ROUND_B = ((12, 6), (8, 4), (4, 2))
+FAR_FIRST = tuple(range(NT // 2, 0, -1)) + tuple(range(-NT // 2 + 1, 0))
+NZ = 8
 
 
 def gather(x, idx):
@@ -91,8 +91,8 @@
 
 
 def kernel(initial, rotation, flips, out, xin, rin, own, own_q, halo, halo_q, fine, fine_q, fine_e, first_run, halo_f,
-           rates, rate_own, rate_ring, start_own, start_ring, ring, ring_e, total, anchor_old, work, term_own, term_in,
-           part_own, part_in, fine_out, load_sem, send_sem, halo_sem, ring_sem, a_sem, b_sem):
+           rates, rate_own, rate_ring, start_own, start_ring, ring, ring_e, total, anchor_old, work, term_own, term_ring,
+           powers, power_in, fine_out, load_sem, send_sem, halo_sem, ring_sem, power_sem, near_sem):
     k = lax.axis_index("tm")
     t = lax.axis_index("tile")
     lane = lax.broadcasted_iota(jnp.int32, (8, 128), 1)
@@ -109,15 +109,18 @@
     barrier = pltpu.get_barrier_semaphore()
     for o in range(1, NT):
         pl.semaphore_signal(barrier, inc=1, device_id=(k, tile_at(o)), device_id_type=MESH)
-    expected = NT - 1
-    for distance, reach in ROUND_A + ROUND_B:
-        @pl.when(k >= distance)
-        def _(distance=distance, reach=reach):
-            for o in range(-reach, reach + 1):
-                pl.semaphore_signal(barrier, inc=1, device_id=(k - distance, tile_at(o)), device_id_type=MESH)
-
-        expected = expected + jnp.where(k + distance < NK, 2 * reach + 1, 0)
-
+    slab, z = k // NZ, lax.rem(k, NZ)
+
+    def slice_at(o):
+        return slab * NZ + lax.rem(z + (o + NZ), NZ)
+
+    across = lax.rem(slab + 1, 2) * NZ + z
+
+    def meet(sem, slices):
+        for other in slices:
+            pl.semaphore_signal(sem, inc=1, device_id=(other, t), device_id_type=MESH)
+
+    meet(barrier, (slice_at(1), slice_at(-1), across))
     odd = {0: None}
     up = down = jnp.int32(0)
     for o in range(1, NT // 2 + 1):
@@ -176,11 +179,12 @@
 
             spread(lambda s, f=f, b=b: xin[f, 8 * b : 8 * b + 8, 128 * s : 128 * s + 128], store_x)
 
-    pl.semaphore_wait(barrier, expected)
-
-    def send(src, dst, recv, where):
+    pl.semaphore_wait(barrier, NT + 2)
+    meet(near_sem.at[0], (slice_at(1), slice_at(-1)))
+
+    def send(src, dst, recv, where, group=0):
         pltpu.make_async_remote_copy(
-            src_ref=src, dst_ref=dst, send_sem=send_sem, recv_sem=recv, device_id=where, device_id_type=MESH
+            src_ref=src, dst_ref=dst, send_sem=send_sem.at[group], recv_sem=recv, device_id=where, device_id_type=MESH
         ).start()
 
     def take(ref, sem):
@@ -191,8 +195,8 @@
     send(own_q.at[:, pl.ds(16, 16), :], halo_q.at[0], halo_sem.at[2], (k, tile_at(1)))
     send(own_q.at[:, pl.ds(0, 16), :], halo_q.at[1], halo_sem.at[3], (k, tile_at(-1)))
     rate_own[...] = restrict(own_q, 0) * 0.25
-    for o in range(1, NT):
-        send(rate_own, rate_ring.at[NT - o - 1], ring_sem.at[0], (k, tile_at(o)))
+    for o in FAR_FIRST:
+        send(rate_own, rate_ring.at[(NT - o) % NT - 1], ring_sem.at[0], (k, tile_at(o)))
 
     take(halo_q.at[0], halo_sem.at[2])
     take(halo_q.at[1], halo_sem.at[3])
@@ -212,6 +216,8 @@
                         fine[f, c, row + 8 * b : row + 8 * b + 8, :] = turn(x, o, f == 2, y)
 
     fill_rims(halo, halo_sem)
+    pl.semaphore_wait(near_sem.at[0], 2)
+    meet(near_sem.at[1], (slice_at(2), slice_at(-2)))
     for f in range(3):
         for half in range(2):
             work[f, pl.ds(CC - 4 + 8 * half, 8), :] = restrict(fine.at[f], FC - 16 + 32 * half) * 0.0625
@@ -221,8 +227,8 @@
         start = restrict(fine.at[f], FC) * 0.0625 - anchor_old[f]
         start_own[f] = start
         ring[f, CC : CC + 8, :] = start
-    for o in range(1, NT):
-        send(start_own, start_ring.at[NT - o - 1], ring_sem.at[1], (k, tile_at(o)))
+    for o in FAR_FIRST:
+        send(start_own, start_ring.at[(NT - o) % NT - 1], ring_sem.at[1], (k, tile_at(o)))
     for f in range(3):
         for c in range(4):
             first_run[f, c] = fine[f, c, FC : FC + 32, :]
@@ -243,6 +249,8 @@
         for f, x in enumerate(oriented(start_ring.at[(o + NT) % NT - 1], o)):
             ring[f, CC + 8 * o : CC + 8 * o + 8, :] = x
 
+    pl.semaphore_wait(near_sem.at[1], 2)
+    meet(near_sem.at[2], (across,))
     for m in (3, 2, 1, 0):
         def chain(s, carry, m=m):
             coarse(ring, ring_e, rates, CC - 16 - 16 * m, 40 + 32 * m)
@@ -253,6 +261,7 @@
         lax.fori_loop(0, jnp.clip(k - 1 - 4 * m, 0, 4), chain, 0)
 
     fill_rims(halo_f, halo_sem.at[pl.ds(4, 2)])
+
     for f in range(3):
         more = total[f]
         for c in range(4):
@@ -277,78 +286,67 @@
         total[f, 0:8, :] = mean
         term_own[f] = start_own_f
 
-    def places(stages):
-        at, base = {}, 0
-        for distance, reach in stages:
-            at[distance] = base
-            base += 2 * reach + 1
-        return at
-
-    def prefix(stages, src, landing, sems, applications):
-        at = places(stages)
-        for stage, (distance, reach) in reversed(list(enumerate(stages))):
-            @pl.when(k + distance < NK)
-            def _(stage=stage, distance=distance, reach=reach):
-                for o in range(-reach, reach + 1):
-                    send(src, landing.at[at[distance] + reach - o], sems.at[stage], (k + distance, tile_at(o)))
-
-        for stage, (distance, reach) in enumerate(stages):
-            @pl.when(k >= distance)
-            def _(stage=stage, distance=distance, reach=reach):
-                base = at[distance]
-                take(landing.at[pl.ds(base, 2 * reach + 1)], sems.at[stage])
-                for o in range(-reach, reach + 1):
-                    for f, x in enumerate(oriented(landing.at[base + reach + o], o)):
-                        rows = slice(CC + 8 * o, CC + 8 * o + 8)
-                        work[f, rows, :] = work[f, rows, :] + x
-                if applications == 1:
-                    coarse(work, ring_e, rates, CC - 4 * (distance - 1), 8 * distance)
-                else:
-                    def apply(s, carry):
-                        coarse(work, ring_e, rates, CC - 4 * (distance - 1), 8 * distance)
-                        return carry
-
-                    lax.fori_loop(0, applications, apply, 0)
-
-    def clear():
-        for f in range(3):
-            for b in range(CR // 8):
-                work[f, 8 * b : 8 * b + 8, :] = zero
-
-    clear()
-    prefix(ROUND_A, term_own, term_in, a_sem, 1)
-    for f in range(3):
-        part_own[f] = work[f, CC : CC + 8, :] + term_own[f]
-    clear()
-    prefix(ROUND_B, part_own, part_in, b_sem, 4)
+    for o in FAR_FIRST:
+        send(term_own, term_ring.at[(NT - o) % NT - 1], ring_sem.at[2], (k, tile_at(o)), 1)
 
     apart_out = lane // 4
     phase = lax.rem(lane, 4)
     for f in range(3):
-        extra = work[f, CC : CC + 8, :] + part_own[f] - total[f, 0:8, :]
-        for c in range(4):
-            for j in range(4):
-                rows = pl.ds(FC + j, 8, stride=4)
-                fine[f, c, rows, :] = fine[f, c, rows, :] + extra
         for b in range(4):
-            z = [fine[f, c, FC + 8 * b : FC + 8 * b + 8, :] for c in range(4)]
+            x = [fine[f, c, FC + 8 * b : FC + 8 * b + 8, :] for c in range(4)]
             for s in range(4):
-                y = [gather(z[c], apart_out + 32 * s) for c in range(4)]
-                out[0, f, 8 * b : 8 * b + 8, 128 * s : 128 * s + 128] = jnp.where(
+                y = [gather(x[c], apart_out + 32 * s) for c in range(4)]
+                fine_out[f, s, 8 * b : 8 * b + 8, :] = jnp.where(
                     phase < 2, jnp.where(phase == 0, y[0], y[1]), jnp.where(phase == 2, y[2], y[3])
                 )
 
+    for f in range(3):
+        work[f, CC : CC + 8, :] = term_own[f]
+    take(term_ring, ring_sem.at[2])
+    for o in offsets:
+        for f, x in enumerate(oriented(term_ring.at[(o + NT) % NT - 1], o)):
+            work[f, CC + 8 * o : CC + 8 * o + 8, :] = x
+    pl.semaphore_wait(near_sem.at[2], 1)
+
+    last = NK - 1 - k
+    m = jnp.int32(0)
+    for group in (3, 2, 1, 0):
+        def power(s, m, group=group):
+            coarse(work, ring_e, rates, CC - 12 - 16 * group, 32 + 32 * group)
+            powers[m] = work[:, CC : CC + 8, :]
+            send(powers.at[m], power_in.at[m], power_sem.at[m], (k + m + 1, t), 2)
+            return m + 1
+
+        m = lax.fori_loop(0, jnp.clip(last - 4 * group, 0, 4), power, m)
+
+    def add(m, carry):
+        take(power_in.at[m], power_sem.at[m])
+        term_own[...] = term_own[...] + power_in[m]
+        return carry
+
+    take(term_ring, send_sem.at[1])
+    lax.fori_loop(0, k, add, 0)
+
+    for f in range(3):
+        extra = term_own[f] - total[f, 0:8, :]
+        for s in range(4):
+            more = gather(extra, apart_out + 32 * s)
+            for j in range(4):
+                rows = pl.ds(j, 8, stride=4)
+                fine_out[f, s, rows, :] = fine_out[f, s, rows, :] + more
+            out[0, f, :, 128 * s : 128 * s + 128] = fine_out[f, s]
+
     for _ in range(2):
-        take(halo, send_sem)
-    take(halo_q, send_sem)
-    take(rate_ring, send_sem)
-    take(start_ring, send_sem)
-    for stages, landing in ((ROUND_A, term_in), (ROUND_B, part_in)):
-        at = places(stages)
-        for distance, reach in stages:
-            @pl.when(k + distance < NK)
-            def _(landing=landing, base=at[distance], count=2 * reach + 1):
-                take(landing.at[pl.ds(base, count)], send_sem)
+        take(halo, send_sem.at[0])
+    take(halo_q, send_sem.at[0])
+    take(rate_ring, send_sem.at[0])
+    take(start_ring, send_sem.at[0])
+
+    def sent(m, carry):
+        take(powers.at[m], send_sem.at[2])
+        return carry
+
+    lax.fori_loop(0, last, sent, 0)
 
 
 def body(initial, rotation, seam_flip):
@@ -367,10 +365,10 @@
         vmem(3, CR, 128), vmem(CR, 128),
         vmem(3, 16, 128), vmem(3, 8, 128),
         vmem(3, CR, 128),
-        vmem(3, 8, 128), vmem(11, 3, 8, 128),
-        vmem(3, 8, 128), vmem(27, 3, 8, 128),
-        vmem(8, 128),
-        dma((2,)), dma, dma((6,)), dma((2,)), dma((3,)), dma((3,)),
+        vmem(3, 8, 128), vmem(NT - 1, 3, 8, 128),
+        vmem(NK - 1, 3, 8, 128), vmem(NK - 1, 3, 8, 128),
+        vmem(3, 4, 32, 128),
+        dma((2,)), dma((3,)), dma((6,)), dma((3,)), dma((NK - 1,)), pltpu.SemaphoreType.REGULAR((3,)),
     ]
     return pl.pallas_call(
         kernel,
@@ -383,7 +381,7 @@
         out_specs=pl.BlockSpec(memory_space=pltpu.VMEM),
         scratch_shapes=scratch,
         compiler_params=pltpu.CompilerParams(
-            collective_id=0, has_side_effects=True, vmem_limit_bytes=24 * 1024 * 1024
+            collective_id=0, has_side_effects=True, vmem_limit_bytes=60 * 1024 * 1024
         ),
         name="parareal",
     )(initial, rotation, seam_flip)

time: 53.1 us -> 37.1 us (0.70); the launches traced: 52.5 us -> 37 us
  Pallas kernels: 49.3 us -> 35.4 us
  local copies, waits for them, and re-layouts: 3.1 us -> 1.62 us
    pallas_call x1, Pallas kernels: 49.3 us -> 35.4 us  [body(): pl.pallas_call(kernel, out_shape=jax.ShapeDtypeStruct((1, 3, 32, 512), jn...]
    unnamed x7 -> x1, local copies, waits for them, and re-layouts: 3.1 us -> 1.62 us
where the time goes in v2:
time: 37.1 us; the launch traced here: 37 us
  Pallas kernels  35.4 us (95%)
  local copies, waits for them, and re-layouts  1.62 us (4%)
    pallas_call x1, Pallas kernels, body(): pl.pallas_call(kernel, out_shape=jax.ShapeDtypeStruct((1, 3, 32, 512), jn...  35.4 us
    unnamed x1, local copies, waits for them, and re-layouts  1.62 us

profile of v2, /device:TPU:4, one launch (start us, length us, event | category | flops | bytes accessed | tf_op | source)
XLA Modules:
  0.0 37.0 jit_solution(6898575796502115164)
XLA Ops:
  0.0 35.4 %parareal.1 = f32[1,3,32,512]{3,2,1,0:T(8,128)} custom-call(f32[3,32,512]{2,1,0:T(8,128)} %initial.1, f32[32,512]{1,0:T(8,128)} %rotation.1, s32[16]{0:T(128)} %flips.1), custom_call_target="tpu_custom_call" | custom-call | tf_op jit(solution)/shard_map/parareal/pallas_call | solution.py:373
  35.4 1.6 %copy.5 = f32[1,3,32,512]{3,2,1,0:T(8,128)} copy(f32[1,3,32,512]{3,2,1,0:T(8,128)} %parareal.1) | data formatting | bytes 393216

commit v3 on v2

--- a/solution.py
+++ b/solution.py
@@ -13,8 +13,8 @@
 FR = 88
 CC = 80
 CR = 168
-FAR_FIRST = tuple(range(NT // 2, 0, -1)) + tuple(range(-NT // 2 + 1, 0))
 NZ = 8
+OTHERS = tuple((x, y, c) for y in (2, 1, 3, 0) for x in (1, 0) for c in (1, 0) if (x, y, c) != (0, 0, 0))
 
 
 def gather(x, idx):
@@ -106,21 +106,24 @@
     load_x.start()
     load_q.start()
 
+    at_xh, at_z = k // NZ, lax.rem(k, NZ)
+    at_xl, at_y, at_core = t // 8, lax.rem(t // 2, 4), lax.rem(t, 2)
+
+    def place(dx=0, dy=0, dz=0, dc=0):
+        px = lax.rem(2 * at_xh + at_xl + (dx + 4), 4)
+        return (
+            (px // 2) * NZ + lax.rem(at_z + (dz + NZ), NZ),
+            lax.rem(px, 2) * 8 + lax.rem(at_y + (dy + 4), 4) * 2 + lax.rem(at_core + dc, 2),
+        )
+
+    def meet(sem, *where):
+        for there in where:
+            pl.semaphore_signal(sem, inc=1, device_id=there, device_id_type=MESH)
+
     barrier = pltpu.get_barrier_semaphore()
-    for o in range(1, NT):
-        pl.semaphore_signal(barrier, inc=1, device_id=(k, tile_at(o)), device_id_type=MESH)
-    slab, z = k // NZ, lax.rem(k, NZ)
-
-    def slice_at(o):
-        return slab * NZ + lax.rem(z + (o + NZ), NZ)
-
-    across = lax.rem(slab + 1, 2) * NZ + z
-
-    def meet(sem, slices):
-        for other in slices:
-            pl.semaphore_signal(sem, inc=1, device_id=(other, t), device_id_type=MESH)
-
-    meet(barrier, (slice_at(1), slice_at(-1), across))
+    beside = (place(dy=1), place(dy=-1), place(dx=1), place(dx=-1), place(dz=1), place(dz=-1))
+    meet(barrier, (k, tile_at(1)), (k, tile_at(-1)), *beside)
+
     odd = {0: None}
     up = down = jnp.int32(0)
     for o in range(1, NT // 2 + 1):
@@ -179,8 +182,7 @@
 
             spread(lambda s, f=f, b=b: xin[f, 8 * b : 8 * b + 8, 128 * s : 128 * s + 128], store_x)
 
-    pl.semaphore_wait(barrier, NT + 2)
-    meet(near_sem.at[0], (slice_at(1), slice_at(-1)))
+    pl.semaphore_wait(barrier, 8)
 
     def send(src, dst, recv, where, group=0):
         pltpu.make_async_remote_copy(
@@ -194,9 +196,43 @@
     send(own.at[:, :, pl.ds(0, 16), :], halo.at[1], halo_sem.at[1], (k, tile_at(-1)))
     send(own_q.at[:, pl.ds(16, 16), :], halo_q.at[0], halo_sem.at[2], (k, tile_at(1)))
     send(own_q.at[:, pl.ds(0, 16), :], halo_q.at[1], halo_sem.at[3], (k, tile_at(-1)))
+    meet(near_sem.at[0], place(dc=1), *beside)
     rate_own[...] = restrict(own_q, 0) * 0.25
-    for o in FAR_FIRST:
-        send(rate_own, rate_ring.at[(NT - o) % NT - 1], ring_sem.at[0], (k, tile_at(o)))
+    pl.semaphore_wait(near_sem.at[0], 7)
+    meet(near_sem.at[1], place(dy=2), place(dc=1), place(dx=2), place(dz=2), place(dz=-2))
+
+    first_blocks = (k + 3) // 4
+    last_blocks = (NK + 2 - k) // 4
+    rate_blocks = jnp.maximum(first_blocks, last_blocks)
+
+    def share(src, landing, sems, blocks, group):
+        for dx, dy, dc in OTHERS:
+            there = lax.rem(at_xl + dx, 2) * 8 + lax.rem(at_y + dy, 4) * 2 + lax.rem(at_core + dc, 2)
+            delta = lax.rem(there - t + NT, NT)
+            far = jnp.minimum(delta, NT - delta)
+            slot = 2 * (far - 1) + jnp.where(delta < 8, 1, 0)
+
+            @pl.when((far - 1) // 2 < blocks)
+            def _(there=there, far=far, slot=slot):
+                send(src, landing.at[slot], sems.at[(far - 1) // 2], (k, there), group)
+
+    def block(landing, b):
+        return landing.at[pl.ds(4 * b, min(4, NT - 1 - 4 * b))]
+
+    def arrive(landing, sems, blocks, use):
+        for b in range(4):
+            @pl.when(b < blocks)
+            def _(b=b):
+                take(block(landing, b), sems.at[b])
+                for a in (2 * b + 1, 2 * b + 2):
+                    use(a, landing.at[2 * a - 2])
+                    use(-a, landing.at[2 * a - 2 + (a < NT // 2)])
+
+    def all_sent(landing, group, blocks):
+        for b in range(4):
+            @pl.when(b < blocks)
+            def _(b=b):
+                take(block(landing, b), send_sem.at[group])
 
     take(halo_q.at[0], halo_sem.at[2])
     take(halo_q.at[1], halo_sem.at[3])
@@ -216,8 +252,9 @@
                         fine[f, c, row + 8 * b : row + 8 * b + 8, :] = turn(x, o, f == 2, y)
 
     fill_rims(halo, halo_sem)
-    pl.semaphore_wait(near_sem.at[0], 2)
-    meet(near_sem.at[1], (slice_at(2), slice_at(-2)))
+    pl.semaphore_wait(near_sem.at[1], 5)
+    meet(near_sem.at[2], place(dx=2))
+    share(rate_own, rate_ring, ring_sem.at[0], rate_blocks, 0)
     for f in range(3):
         for half in range(2):
             work[f, pl.ds(CC - 4 + 8 * half, 8), :] = restrict(fine.at[f], FC - 16 + 32 * half) * 0.0625
@@ -227,30 +264,32 @@
         start = restrict(fine.at[f], FC) * 0.0625 - anchor_old[f]
         start_own[f] = start
         ring[f, CC : CC + 8, :] = start
-    for o in FAR_FIRST:
-        send(start_own, start_ring.at[(NT - o) % NT - 1], ring_sem.at[1], (k, tile_at(o)))
+    share(start_own, start_ring, ring_sem.at[1], first_blocks, 1)
     for f in range(3):
         for c in range(4):
             first_run[f, c] = fine[f, c, FC : FC + 32, :]
     send(first_run.at[:, :, pl.ds(16, 16), :], halo_f.at[0], halo_sem.at[4], (k, tile_at(1)))
     send(first_run.at[:, :, pl.ds(0, 16), :], halo_f.at[1], halo_sem.at[5], (k, tile_at(-1)))
 
-    offsets = [o for o in range(-(NT // 2), NT // 2 + 1) if o]
-    take(rate_ring, ring_sem.at[0])
     rates[CC : CC + 8, :] = rate_own[...]
-    for o in offsets:
-        rates[CC + 8 * o : CC + 8 * o + 8, :] = turn(rate_ring[(o + NT) % NT - 1], o, True)
+
+    def use_rate(o, ref):
+        rates[CC + 8 * o : CC + 8 * o + 8, :] = turn(ref[...], o, True)
+
+    arrive(rate_ring, ring_sem.at[0], rate_blocks, use_rate)
     coarse(work, ring_e, rates, CC, 8)
     for f in range(3):
         anchor_old[f] = work[f, CC : CC + 8, :]
 
-    take(start_ring, ring_sem.at[1])
-    for o in offsets:
-        for f, x in enumerate(oriented(start_ring.at[(o + NT) % NT - 1], o)):
-            ring[f, CC + 8 * o : CC + 8 * o + 8, :] = x
-
-    pl.semaphore_wait(near_sem.at[1], 2)
-    meet(near_sem.at[2], (across,))
+    def use_in(whole):
+        def use(o, ref):
+            for f, x in enumerate(oriented(ref, o)):
+                whole[f, CC + 8 * o : CC + 8 * o + 8, :] = x
+
+        return use
+
+    arrive(start_ring, ring_sem.at[1], first_blocks, use_in(ring))
+
     for m in (3, 2, 1, 0):
         def chain(s, carry, m=m):
             coarse(ring, ring_e, rates, CC - 16 - 16 * m, 40 + 32 * m)
@@ -286,8 +325,7 @@
         total[f, 0:8, :] = mean
         term_own[f] = start_own_f
 
-    for o in FAR_FIRST:
-        send(term_own, term_ring.at[(NT - o) % NT - 1], ring_sem.at[2], (k, tile_at(o)), 1)
+    share(term_own, term_ring, ring_sem.at[2], last_blocks, 2)
 
     apart_out = lane // 4
     phase = lax.rem(lane, 4)
@@ -302,10 +340,7 @@
 
     for f in range(3):
         work[f, CC : CC + 8, :] = term_own[f]
-    take(term_ring, ring_sem.at[2])
-    for o in offsets:
-        for f, x in enumerate(oriented(term_ring.at[(o + NT) % NT - 1], o)):
-            work[f, CC + 8 * o : CC + 8 * o + 8, :] = x
+    arrive(term_ring, ring_sem.at[2], last_blocks, use_in(work))
     pl.semaphore_wait(near_sem.at[2], 1)
 
     last = NK - 1 - k
@@ -314,7 +349,7 @@
         def power(s, m, group=group):
             coarse(work, ring_e, rates, CC - 12 - 16 * group, 32 + 32 * group)
             powers[m] = work[:, CC : CC + 8, :]
-            send(powers.at[m], power_in.at[m], power_sem.at[m], (k + m + 1, t), 2)
+            send(powers.at[m], power_in.at[m], power_sem.at[m], (k + m + 1, t), 3)
             return m + 1
 
         m = lax.fori_loop(0, jnp.clip(last - 4 * group, 0, 4), power, m)
@@ -324,7 +359,7 @@
         term_own[...] = term_own[...] + power_in[m]
         return carry
 
-    take(term_ring, send_sem.at[1])
+    all_sent(term_ring, 2, last_blocks)
     lax.fori_loop(0, k, add, 0)
 
     for f in range(3):
@@ -339,11 +374,11 @@
     for _ in range(2):
         take(halo, send_sem.at[0])
     take(halo_q, send_sem.at[0])
-    take(rate_ring, send_sem.at[0])
-    take(start_ring, send_sem.at[0])
+    all_sent(rate_ring, 0, rate_blocks)
+    all_sent(start_ring, 1, first_blocks)
 
     def sent(m, carry):
-        take(powers.at[m], send_sem.at[2])
+        take(powers.at[m], send_sem.at[3])
         return carry
 
     lax.fori_loop(0, last, sent, 0)
@@ -368,7 +403,7 @@
         vmem(3, 8, 128), vmem(NT - 1, 3, 8, 128),
         vmem(NK - 1, 3, 8, 128), vmem(NK - 1, 3, 8, 128),
         vmem(3, 4, 32, 128),
-        dma((2,)), dma((3,)), dma((6,)), dma((3,)), dma((NK - 1,)), pltpu.SemaphoreType.REGULAR((3,)),
+        dma((2,)), dma((4,)), dma((6,)), dma((3, 4)), dma((NK - 1,)), pltpu.SemaphoreType.REGULAR((3,)),
     ]
     return pl.pallas_call(
         kernel,

time: 37.1 us -> 35 us (0.943); the launches traced: 37 us -> 34.3 us
  Pallas kernels: 35.4 us -> 32.7 us
    pallas_call x1, Pallas kernels: 35.4 us -> 32.7 us  [body(): pl.pallas_call(kernel, out_shape=jax.ShapeDtypeStruct((1, 3, 32, 512), jn...]
where the time goes in v3:
time: 35 us; the launch traced here: 34.3 us
  Pallas kernels  32.7 us (93%)
  local copies, waits for them, and re-layouts  1.62 us (5%)
    pallas_call x1, Pallas kernels, body(): pl.pallas_call(kernel, out_shape=jax.ShapeDtypeStruct((1, 3, 32, 512), jn...  32.7 us
    unnamed x1, local copies, waits for them, and re-layouts  1.62 us

profile of v3, /device:TPU:4, one launch (start us, length us, event | category | flops | bytes accessed | tf_op | source)
XLA Modules:
  0.0 34.3 jit_solution(3814034409980881963)
XLA Ops:
  0.0 32.7 %parareal.1 = f32[1,3,32,512]{3,2,1,0:T(8,128)} custom-call(f32[3,32,512]{2,1,0:T(8,128)} %initial.1, f32[32,512]{1,0:T(8,128)} %rotation.1, s32[16]{0:T(128)} %flips.1), custom_call_target="tpu_custom_call" | custom-call | tf_op jit(solution)/shard_map/parareal/pallas_call | solution.py:408
  32.7 1.6 %copy.5 = f32[1,3,32,512]{3,2,1,0:T(8,128)} copy(f32[1,3,32,512]{3,2,1,0:T(8,128)} %parareal.1) | data formatting | bytes 393216

commit v4 on v3

v4 whole, which is shorter than its diff:
```python
import jax
import jax.numpy as jnp
from jax import lax
from jax.experimental import pallas as pl
from jax.experimental.pallas import tpu as pltpu
from jax.sharding import PartitionSpec as P

MESH = pl.DeviceIdType.MESH
NT = 16
NK = 16
HC = 0.45
FC = 24
FR = 88
CC = 80
CR = 168
NZ = 8
OTHERS = tuple((x, y, c) for y in (2, 1, 3, 0) for x in (1, 0) for c in (1, 0) if (x, y, c) != (0, 0, 0))


def gather(x, idx):
    return jnp.take_along_axis(x, idx, axis=1)


def ahead(x):
    return pltpu.roll(x, 127, 1)


def behind(x):
    return pltpu.roll(x, 1, 1)


def blocks(first, past):
    return range(first // 8 * 8, -(-past // 8) * 8, 8)


def coarse_step(st, e_ref, q, first, past):
    for r in blocks(first - 1, past + 1):
        g = st[0, r : r + 8, :] - HC * (st[1, r + 1 : r + 9, :] - st[1, r - 1 : r + 7, :])
        v = st[2, r : r + 8, :]
        wide = pltpu.roll(v, 126, 1) - 2.0 * v + pltpu.roll(v, 2, 1)
        st[0, r : r + 8, :] = g - HC * (ahead(v) - behind(v))
        e_ref[r : r + 8, :] = HC * ((ahead(g) - behind(g)) - HC * wide)
    for r in blocks(first, past):
        u, v, rate = st[1, r : r + 8, :], st[2, r : r + 8, :], q[r : r + 8, :]
        new = u + rate * v - HC * (st[0, r + 1 : r + 9, :] - st[0, r - 1 : r + 7, :])
        st[1, r : r + 8, :] = new
        st[2, r : r + 8, :] = v - rate * new - e_ref[r : r + 8, :]


def coarse(st, e_ref, q, first, past):
    coarse_step(st, e_ref, q, first - 2, past + 2)
    coarse_step(st, e_ref, q, first, past)


def fine_step(st, e_ref, q, first, past):
    for r in blocks(first - 1, past + 1):
        v = [st[2, c, r : r + 8, :] for c in range(4)]
        g = [st[0, c, r : r + 8, :] - HC * (st[1, c, r + 1 : r + 9, :] - st[1, c, r - 1 : r + 7, :]) for c in range(4)]
        vs = [behind(v[2]), behind(v[3])] + v + [ahead(v[0]), ahead(v[1])]
        gs = [behind(g[3])] + g + [ahead(g[0])]
        for c in range(4):
            st[0, c, r : r + 8, :] = g[c] - HC * (vs[c + 3] - vs[c + 1])
            e_ref[c, r : r + 8, :] = HC * ((gs[c + 2] - gs[c]) - HC * (vs[c + 4] - 2.0 * v[c] + vs[c]))
    for r in blocks(first, past):
        for c in range(4):
            u, v, rate = st[1, c, r : r + 8, :], st[2, c, r : r + 8, :], q[c, r : r + 8, :]
            new = u + rate * v - HC * (st[0, c, r + 1 : r + 9, :] - st[0, c, r - 1 : r + 7, :])
            st[1, c, r : r + 8, :] = new
            st[2, c, r : r + 8, :] = v - rate * new - e_ref[c, r : r + 8, :]


def fine_run(st, e_ref, q):
    for s in range(8):
        fine_step(st, e_ref, q, FC - 14 + 2 * s, FC + 46 - 2 * s)


def restrict(ref, first):
    total = None
    for j in range(4):
        for c in range(4):
            part = ref[c, pl.ds(first + j, 8, stride=4), :]
            total = part if total is None else total + part
    return total


def kernel(initial, rotation, flips, out, xin, rin, own, own_q, halo, halo_q, fine, fine_q, fine_e, first_run, halo_f,
           rates, rate_own, rate_ring, start_own, start_ring, ring, ring_e, total, total_j, total_k, first_end, work, term_own, term_ring,
           powers, power_in, fine_out, load_sem, send_sem, halo_sem, ring_sem, power_sem, near_sem):
    k = lax.axis_index("tm")
    t = lax.axis_index("tile")
    lane = lax.broadcasted_iota(jnp.int32, (8, 128), 1)
    turned = 127 - lane

    def tile_at(o):
        return lax.rem(t + (o + NT), NT)

    load_x = pltpu.make_async_copy(initial, xin, load_sem.at[0])
    load_q = pltpu.make_async_copy(rotation, rin, load_sem.at[1])
    load_x.start()
    load_q.start()

    at_xh, at_z = k // NZ, lax.rem(k, NZ)
    at_xl, at_y, at_core = t // 8, lax.rem(t // 2, 4), lax.rem(t, 2)

    def place(dx=0, dy=0, dz=0, dc=0):
        px = lax.rem(2 * at_xh + at_xl + (dx + 4), 4)
        return (
            (px // 2) * NZ + lax.rem(at_z + (dz + NZ), NZ),
            lax.rem(px, 2) * 8 + lax.rem(at_y + (dy + 4), 4) * 2 + lax.rem(at_core + dc, 2),
        )

    def meet(sem, *where):
        for there in where:
            pl.semaphore_signal(sem, inc=1, device_id=there, device_id_type=MESH)

    barrier = pltpu.get_barrier_semaphore()
    meet(barrier, *((k, tile_at(o)) for o in (1, -1, 8, 4, -4, 2, -2, 3, -3, 5, -5, 6, -6, 7, -7)), place(dx=2))
    for dz in range(1, NZ):
        @pl.when(at_z + dz < NZ)
        def _(dz=dz):
            meet(barrier, (at_z + dz, t), (NZ + at_z + dz, t))

    j = jnp.where(k < 4, jnp.where(k == 0, 8, k), jnp.where(k < 8, jnp.where(k == 4, 0, k + 4), jnp.where(k < 12, k - 4, k)))
    n = jnp.maximum(j, k)

    odd = {0: None}
    up = down = jnp.int32(0)
    for o in range(1, NT // 2 + 1):
        up = up + jnp.where(flips[tile_at(o)] != 0, 1, 0)
        down = down + jnp.where(flips[tile_at(1 - o)] != 0, 1, 0)
        odd[o] = (jnp.zeros((8, 128), jnp.int32) + lax.rem(up, 2)) != 0
        odd[-o] = (jnp.zeros((8, 128), jnp.int32) + lax.rem(down, 2)) != 0

    def turn(x, o, negate, other=None):
        if o == 0:
            return x
        back = gather(x if other is None else other, turned)
        return jnp.where(odd[o], -back if negate else back, x)

    def oriented(src, o):
        return [turn(src[f], o, f == 2) for f in range(3)]

    zero = jnp.zeros((8, 128), jnp.float32)
    for f in range(3):
        for b in range(CR // 8):
            work[f, 8 * b : 8 * b + 8, :] = zero
        for b in (0, 1, CR // 8 - 2, CR // 8 - 1):
            ring[f, 8 * b : 8 * b + 8, :] = zero
        for c in range(4):
            for b in (0, FR // 8 - 2, FR // 8 - 1):
                fine[f, c, 8 * b : 8 * b + 8, :] = zero
        for ref in (total, total_j, total_k):
            ref[f] = jnp.zeros((16, 128), jnp.float32)
    for b in (0, 1, CR // 8 - 2, CR // 8 - 1):
        rates[8 * b : 8 * b + 8, :] = zero
    for c in range(4):
        for b in (0, FR // 8 - 2, FR // 8 - 1):
            fine_q[c, 8 * b : 8 * b + 8, :] = zero

    quarter = lane // 32
    apart = 4 * lax.rem(lane, 32)

    def spread(load, store):
        x = [load(s) for s in range(4)]
        for c in range(4):
            y = [gather(x[s], apart + c) for s in range(4)]
            store(c, jnp.where(quarter < 2, jnp.where(quarter == 0, y[0], y[1]), jnp.where(quarter == 2, y[2], y[3])))

    load_q.wait()
    for b in range(4):
        def store_q(c, x, b=b):
            own_q[c, 8 * b : 8 * b + 8, :] = x
            fine_q[c, FC + 8 * b : FC + 8 * b + 8, :] = x

        spread(lambda s, b=b: rin[8 * b : 8 * b + 8, 128 * s : 128 * s + 128], store_q)
    load_x.wait()
    for f in range(3):
        for b in range(4):
            def store_x(c, x, f=f, b=b):
                own[f, c, 8 * b : 8 * b + 8, :] = x
                fine[f, c, FC + 8 * b : FC + 8 * b + 8, :] = x

            spread(lambda s, f=f, b=b: xin[f, 8 * b : 8 * b + 8, 128 * s : 128 * s + 128], store_x)

    pl.semaphore_wait(barrier, NT + 2 * at_z)

    def send(src, dst, recv, where, group=0):
        pltpu.make_async_remote_copy(
            src_ref=src, dst_ref=dst, send_sem=send_sem.at[group], recv_sem=recv, device_id=where, device_id_type=MESH
        ).start()

    def take(ref, sem):
        pltpu.make_async_copy(ref, ref, sem).wait()

    send(own.at[:, :, pl.ds(16, 16), :], halo.at[0], halo_sem.at[0], (k, tile_at(1)))
    send(own.at[:, :, pl.ds(0, 16), :], halo.at[1], halo_sem.at[1], (k, tile_at(-1)))
    send(own_q.at[:, pl.ds(16, 16), :], halo_q.at[0], halo_sem.at[2], (k, tile_at(1)))
    send(own_q.at[:, pl.ds(0, 16), :], halo_q.at[1], halo_sem.at[3], (k, tile_at(-1)))
    rate_own[...] = restrict(own_q, 0) * 0.25

    first_blocks = (n + 3) // 4
    last_blocks = jnp.where(j == 0, 0, (NK + 2 - j) // 4)
    rate_blocks = jnp.maximum(first_blocks, last_blocks)

    def share(src, landing, sems, count, group):
        for dx, dy, dc in OTHERS:
            there = lax.rem(at_xl + dx, 2) * 8 + lax.rem(at_y + dy, 4) * 2 + lax.rem(at_core + dc, 2)
            delta = lax.rem(there - t + NT, NT)
            far = jnp.minimum(delta, NT - delta)
            slot = 2 * (far - 1) + jnp.where(delta < 8, 1, 0)

            @pl.when((far - 1) // 2 < count)
            def _(there=there, far=far, slot=slot):
                send(src, landing.at[slot], sems.at[(far - 1) // 2], (k, there), group)

    def block(landing, b):
        return landing.at[pl.ds(4 * b, min(4, NT - 1 - 4 * b))]

    def arrive(landing, sems, count, use):
        for b in range(4):
            @pl.when(b < count)
            def _(b=b):
                take(block(landing, b), sems.at[b])
                for a in (2 * b + 1, 2 * b + 2):
                    use(a, landing.at[2 * a - 2])
                    use(-a, landing.at[2 * a - 2 + (a < NT // 2)])

    def all_sent(landing, group, count):
        for b in range(4):
            @pl.when(b < count)
            def _(b=b):
                take(block(landing, b), send_sem.at[group])

    for dz in range(1, NZ):
        @pl.when(at_z >= dz)
        def _(dz=dz):
            meet(near_sem, (at_z - dz, t), (NZ + at_z - dz, t))

    take(halo_q.at[0], halo_sem.at[2])
    take(halo_q.at[1], halo_sem.at[3])
    for side, o, row in ((0, -1, FC - 16), (1, 1, FC + 32)):
        for b in range(2):
            for c in range(4):
                x, y = (halo_q[side, cc, 8 * b : 8 * b + 8, :] for cc in (c, 3 - c))
                fine_q[c, row + 8 * b : row + 8 * b + 8, :] = turn(x, o, True, y)

    def fill_rims(src, sem):
        for side, o, row in ((0, -1, FC - 16), (1, 1, FC + 32)):
            take(src.at[side], sem.at[side])
            for f in range(3):
                for b in range(2):
                    for c in range(4):
                        x, y = (src[side, f, cc, 8 * b : 8 * b + 8, :] for cc in (c, 3 - c))
                        fine[f, c, row + 8 * b : row + 8 * b + 8, :] = turn(x, o, f == 2, y)

    fill_rims(halo, halo_sem)
    share(rate_own, rate_ring, ring_sem.at[0], rate_blocks, 0)
    fine_run(fine, fine_e, fine_q)
    for f in range(3):
        first_end[f] = restrict(fine.at[f], FC) * 0.0625
        start = first_end[f] - restrict(own.at[f], 0) * 0.0625
        start_own[f] = start
        ring[f, CC : CC + 8, :] = start
        for c in range(4):
            first_run[f, c] = fine[f, c, FC : FC + 32, :]

    def edges():
        send(first_run.at[:, :, pl.ds(16, 16), :], halo_f.at[0], halo_sem.at[4], (k, tile_at(1)))
        send(first_run.at[:, :, pl.ds(0, 16), :], halo_f.at[1], halo_sem.at[5], (k, tile_at(-1)))

    share(start_own, start_ring, ring_sem.at[1], first_blocks, 1)
    edges()

    rates[CC : CC + 8, :] = rate_own[...]

    def use_rate(o, ref):
        rates[CC + 8 * o : CC + 8 * o + 8, :] = turn(ref[...], o, True)

    arrive(rate_ring, ring_sem.at[0], rate_blocks, use_rate)

    def use_in(whole):
        def use(o, ref):
            for f, x in enumerate(oriented(ref, o)):
                whole[f, CC + 8 * o : CC + 8 * o + 8, :] = x

        return use

    arrive(start_ring, ring_sem.at[1], first_blocks, use_in(ring))

    def chain(least, most, i):
        for m in (3, 2, 1, 0):
            def one(_, i, m=m):
                coarse(ring, ring_e, rates, CC - 12 - 16 * m, CC + 20 + 16 * m)
                for f in range(3):
                    total[f] = total[f] + ring[f, pl.ds(CC - 4, 16), :]

                @pl.when(i == j - 1)
                def _():
                    total_j[...] = total[...]

                @pl.when(i == k - 1)
                def _():
                    total_k[...] = total[...]

                return i + 1

            count = jnp.minimum(most, 4 * m + 4) - jnp.maximum(least, 4 * m)
            i = lax.fori_loop(0, jnp.maximum(count, 0), one, i)
        return i

    def fine_from(change):
        for side, o, row in ((0, -1, FC - 16), (1, 1, FC + 32)):
            for f in range(3):
                for b in range(2):
                    for c in range(4):
                        x, y = (halo_f[side, f, cc, 8 * b : 8 * b + 8, :] for cc in (c, 3 - c))
                        fine[f, c, row + 8 * b : row + 8 * b + 8, :] = turn(x, o, f == 2, y)
        for f in range(3):
            more = change[f]
            for c in range(4):
                fine[f, c, FC : FC + 32, :] = first_run[f, c]
                for p in range(4):
                    rows = pl.ds(FC - 16 + p, 16, stride=4)
                    fine[f, c, rows, :] = fine[f, c, rows, :] + more
        fine_run(fine, fine_e, fine_q)

    i = chain(n - j, n, jnp.int32(1))
    take(halo_f.at[0], halo_sem.at[4])
    take(halo_f.at[1], halo_sem.at[5])

    @pl.when(j > 0)
    def _():
        fine_from(total_j)

    for f in range(3):
        term = restrict(fine.at[f], FC) * 0.0625 - (first_end[f] + total[f, 4:12, :])
        term_own[f] = term
        work[f, CC : CC + 8, :] = term
    share(term_own, term_ring, ring_sem.at[2], last_blocks, 2)

    chain(0, n - j, i)

    @pl.when((j != k) & (k > 0))
    def _():
        fine_from(total_k)

    @pl.when(k == 0)
    def _():
        for f in range(3):
            for c in range(4):
                fine[f, c, FC : FC + 32, :] = first_run[f, c]


    apart_out = lane // 4
    phase = lax.rem(lane, 4)
    for f in range(3):
        for b in range(4):
            x = [fine[f, c, FC + 8 * b : FC + 8 * b + 8, :] for c in range(4)]
            for s in range(4):
                y = [gather(x[c], apart_out + 32 * s) for c in range(4)]
                fine_out[f, s, 8 * b : 8 * b + 8, :] = jnp.where(
                    phase < 2, jnp.where(phase == 0, y[0], y[1]), jnp.where(phase == 2, y[2], y[3])
                )

    arrive(term_ring, ring_sem.at[2], last_blocks, use_in(work))

    @pl.when(at_z < NZ - 1)
    def _():
        pl.semaphore_wait(near_sem, 2 * (NZ - 1 - at_z))


    last = jnp.where(j == 0, 0, NK - 1 - j)
    m = jnp.int32(0)
    for group in (3, 2, 1, 0):
        def power(s, m, group=group):
            coarse(work, ring_e, rates, CC - 12 - 16 * group, CC + 20 + 16 * group)
            powers[m] = work[:, CC : CC + 8, :]

            @pl.when(j + m + 1 != k)
            def _():
                send(powers.at[m], power_in.at[m], power_sem.at[m], (j + m + 1, t), 3)

            @pl.when(j + m + 1 == k)
            def _():
                pltpu.make_async_copy(powers.at[m], power_in.at[m], power_sem.at[m]).start()

            return m + 1

        m = lax.fori_loop(0, jnp.clip(last - 4 * group, 0, 4), power, m)

    all_sent(term_ring, 2, last_blocks)
    term_own[...] = jnp.zeros((3, 8, 128), jnp.float32)

    def add(m, carry):
        take(power_in.at[m], power_sem.at[m])
        term_own[...] = term_own[...] + power_in[m]
        return carry

    lax.fori_loop(0, k - 1, add, 0)

    for f in range(3):
        extra = term_own[f]
        for s in range(4):
            more = gather(extra, apart_out + 32 * s)
            for p in range(4):
                rows = pl.ds(p, 8, stride=4)
                fine_out[f, s, rows, :] = fine_out[f, s, rows, :] + more
            out[0, f, :, 128 * s : 128 * s + 128] = fine_out[f, s]

    for _ in range(2):
        take(halo, send_sem.at[0])
    take(halo_q, send_sem.at[0])
    all_sent(rate_ring, 0, rate_blocks)
    all_sent(start_ring, 1, first_blocks)

    def sent(m, carry):
        take(powers.at[m], send_sem.at[3])
        return carry

    lax.fori_loop(0, last - jnp.where((j > 0) & (k > j), 1, 0), sent, 0)


def body(initial, rotation, seam_flip):
    def vmem(*shape):
        return pltpu.VMEM(shape, jnp.float32)

    dma = pltpu.SemaphoreType.DMA
    scratch = [
        vmem(3, 32, 512), vmem(32, 512),
        vmem(3, 4, 32, 128), vmem(4, 32, 128),
        vmem(2, 3, 4, 16, 128), vmem(2, 4, 16, 128),
        vmem(3, 4, FR, 128), vmem(4, FR, 128), vmem(4, FR, 128),
        vmem(3, 4, 32, 128), vmem(2, 3, 4, 16, 128),
        vmem(CR, 128), vmem(8, 128), vmem(NT - 1, 8, 128),
        vmem(3, 8, 128), vmem(NT - 1, 3, 8, 128),
        vmem(3, CR, 128), vmem(CR, 128),
        vmem(3, 16, 128), vmem(3, 16, 128), vmem(3, 16, 128), vmem(3, 8, 128),
        vmem(3, CR, 128),
        vmem(3, 8, 128), vmem(NT - 1, 3, 8, 128),
        vmem(NK - 1, 3, 8, 128), vmem(NK - 1, 3, 8, 128),
        vmem(3, 4, 32, 128),
        dma((2,)), dma((4,)), dma((6,)), dma((3, 4)), dma((NK - 1,)), pltpu.SemaphoreType.REGULAR,
    ]
    return pl.pallas_call(
        kernel,
        out_shape=jax.ShapeDtypeStruct((1, 3, 32, 512), jnp.float32),
        in_specs=[
            pl.BlockSpec(memory_space=pl.ANY),
            pl.BlockSpec(memory_space=pl.ANY),
            pl.BlockSpec(memory_space=pltpu.SMEM),
        ],
        out_specs=pl.BlockSpec(memory_space=pltpu.VMEM),
        scratch_shapes=scratch,
        compiler_params=pltpu.CompilerParams(
            collective_id=0, has_side_effects=True, vmem_limit_bytes=60 * 1024 * 1024
        ),
        name="parareal",
    )(initial, rotation, seam_flip)


def solution(mesh):
    in_specs = (P(None, "tile", None), P("tile", None), P())
    out_specs = P("tm", None, "tile", None)
    return jax.shard_map(body, mesh=mesh, in_specs=in_specs, out_specs=out_specs, check_vma=False)
```

time: 35 us -> 33.2 us (0.949)
  the two profiles are of different devices: /device:TPU:4 before, /device:TPU:70 now
where the time goes in v4:
time: 33.2 us; the launch traced here: 33.1 us
  Pallas kernels  31.5 us (95%)
  local copies, waits for them, and re-layouts  1.62 us (5%)
    pallas_call x1, Pallas kernels, body(): pl.pallas_call(kernel, out_shape=jax.ShapeDtypeStruct((1, 3, 32, 512), jn...  31.5 us
    unnamed x1, local copies, waits for them, and re-layouts  1.62 us

profile of v4, /device:TPU:70, one launch (start us, length us, event | category | flops | bytes accessed | tf_op | source)
XLA Modules:
  0.0 33.1 jit_solution(3630485741528142436)
XLA Ops:
  0.0 31.5 %parareal.1 = f32[1,3,32,512]{3,2,1,0:T(8,128)} custom-call(f32[3,32,512]{2,1,0:T(8,128)} %initial.1, f32[32,512]{1,0:T(8,128)} %rotation.1, s32[16]{0:T(128)} %flips.1), custom_call_target="tpu_custom_call" | custom-call | tf_op jit(solution)/shard_map/parareal/pallas_call | solution.py:444
  31.5 1.6 %copy.5 = f32[1,3,32,512]{3,2,1,0:T(8,128)} copy(f32[1,3,32,512]{3,2,1,0:T(8,128)} %parareal.1) | data formatting | bytes 393216

commit v5 on v4

--- a/solution.py
+++ b/solution.py
@@ -83,7 +83,7 @@
     return total
 
 
-def kernel(initial, rotation, flips, out, xin, rin, own, own_q, halo, halo_q, fine, fine_q, fine_e, first_run, halo_f,
+def kernel(initial, rotation, flips, out, change, xin, rin, own, own_q, halo, halo_q, fine, fine_q, fine_e, first_run, halo_f,
            rates, rate_own, rate_ring, start_own, start_ring, ring, ring_e, total, total_j, total_k, first_end, work, term_own, term_ring,
            powers, power_in, fine_out, load_sem, send_sem, halo_sem, ring_sem, power_sem, near_sem):
     k = lax.axis_index("tm")
@@ -120,7 +120,8 @@
         def _(dz=dz):
             meet(barrier, (at_z + dz, t), (NZ + at_z + dz, t))
 
-    j = jnp.where(k < 4, jnp.where(k == 0, 8, k), jnp.where(k < 8, jnp.where(k == 4, 0, k + 4), jnp.where(k < 12, k - 4, k)))
+    j = jnp.where(k < 4, jnp.where(k == 0, 8, k), jnp.where(k < 8, k + 8, jnp.where(k < 12, k - 4, k - 3)))
+    j = jnp.where(k == 7, 0, jnp.where(k == 15, 15, j))
     n = jnp.maximum(j, k)
 
     odd = {0: None}
@@ -358,10 +359,12 @@
             x = [fine[f, c, FC + 8 * b : FC + 8 * b + 8, :] for c in range(4)]
             for s in range(4):
                 y = [gather(x[c], apart_out + 32 * s) for c in range(4)]
-                fine_out[f, s, 8 * b : 8 * b + 8, :] = jnp.where(
+                fine_out[f, 8 * b : 8 * b + 8, 128 * s : 128 * s + 128] = jnp.where(
                     phase < 2, jnp.where(phase == 0, y[0], y[1]), jnp.where(phase == 2, y[2], y[3])
                 )
 
+    keep = pltpu.make_async_copy(fine_out, out, load_sem.at[0])
+    keep.start()
     arrive(term_ring, ring_sem.at[2], last_blocks, use_in(work))
 
     @pl.when(at_z < NZ - 1)
@@ -398,14 +401,8 @@
 
     lax.fori_loop(0, k - 1, add, 0)
 
-    for f in range(3):
-        extra = term_own[f]
-        for s in range(4):
-            more = gather(extra, apart_out + 32 * s)
-            for p in range(4):
-                rows = pl.ds(p, 8, stride=4)
-                fine_out[f, s, rows, :] = fine_out[f, s, rows, :] + more
-            out[0, f, :, 128 * s : 128 * s + 128] = fine_out[f, s]
+    change[...] = term_own[...]
+    keep.wait()
 
     for _ in range(2):
         take(halo, send_sem.at[0])
@@ -418,6 +415,29 @@
         return carry
 
     lax.fori_loop(0, last - jnp.where((j > 0) & (k > j), 1, 0), sent, 0)
+
+
+def finish(fine, change, out, fine_in, change_in, sems):
+    loads = [pltpu.make_async_copy(fine.at[f], fine_in.at[f], sems.at[f]) for f in range(3)]
+    stores = [pltpu.make_async_copy(fine_in.at[f], out.at[0, f], sems.at[f]) for f in range(3)]
+    load_change = pltpu.make_async_copy(change, change_in, sems.at[3])
+    load_change.start()
+    for load in loads:
+        load.start()
+    load_change.wait()
+    wide = lax.broadcasted_iota(jnp.int32, (8, 128), 1) // 4
+    first = lax.broadcasted_iota(jnp.int32, (8, 128), 0) < 4
+    for f in range(3):
+        more = [gather(change_in[f], wide + 32 * s) for s in range(4)]
+        loads[f].wait()
+        for s in range(4):
+            for b in range(4):
+                upper, lower = (jnp.broadcast_to(more[s][r : r + 1, :], (8, 128)) for r in (2 * b, 2 * b + 1))
+                at = (f, slice(8 * b, 8 * b + 8), slice(128 * s, 128 * s + 128))
+                fine_in[at] = fine_in[at] + jnp.where(first, upper, lower)
+        stores[f].start()
+    for store in stores:
+        store.wait()
 
 
 def body(initial, rotation, seam_flip):
@@ -438,24 +458,36 @@
         vmem(3, CR, 128),
         vmem(3, 8, 128), vmem(NT - 1, 3, 8, 128),
         vmem(NK - 1, 3, 8, 128), vmem(NK - 1, 3, 8, 128),
-        vmem(3, 4, 32, 128),
+        vmem(3, 32, 512),
         dma((2,)), dma((4,)), dma((6,)), dma((3, 4)), dma((NK - 1,)), pltpu.SemaphoreType.REGULAR,
     ]
-    return pl.pallas_call(
+    fine, change = pl.pallas_call(
         kernel,
-        out_shape=jax.ShapeDtypeStruct((1, 3, 32, 512), jnp.float32),
+        out_shape=(
+            jax.ShapeDtypeStruct((3, 32, 512), jnp.float32),
+            jax.ShapeDtypeStruct((3, 8, 128), jnp.float32),
+        ),
         in_specs=[
             pl.BlockSpec(memory_space=pl.ANY),
             pl.BlockSpec(memory_space=pl.ANY),
             pl.BlockSpec(memory_space=pltpu.SMEM),
         ],
-        out_specs=pl.BlockSpec(memory_space=pltpu.VMEM),
+        out_specs=(pl.BlockSpec(memory_space=pl.ANY), pl.BlockSpec(memory_space=pltpu.VMEM)),
         scratch_shapes=scratch,
         compiler_params=pltpu.CompilerParams(
             collective_id=0, has_side_effects=True, vmem_limit_bytes=60 * 1024 * 1024
         ),
         name="parareal",
     )(initial, rotation, seam_flip)
+    return pl.pallas_call(
+        finish,
+        out_shape=jax.ShapeDtypeStruct((1, 3, 32, 512), jnp.float32),
+        in_specs=[pl.BlockSpec(memory_space=pl.ANY)] * 2,
+        out_specs=pl.BlockSpec(memory_space=pl.ANY),
+        scratch_shapes=[vmem(3, 32, 512), vmem(3, 8, 128), dma((4,))],
+        compiler_params=pltpu.CompilerParams(vmem_limit_bytes=60 * 1024 * 1024),
+        name="finish",
+    )(fine, change)
 
 
 def solution(mesh):

time: 33.2 us -> 32.3 us (0.973)
  the two profiles are of different devices: /device:TPU:70 before, /device:TPU:4 now
where the time goes in v5:
time: 32.3 us; the launch traced here: 31.8 us
  Pallas kernels  31.8 us (98%)
    pallas_call x1, Pallas kernels, body(): pl.pallas_call(kernel, out_shape=(jax.ShapeDtypeStruct((3, 32, 512), jnp....  30.1 us
    pallas_call x1, Pallas kernels, body(): pl.pallas_call(finish, out_shape=jax.ShapeDtypeStruct((1, 3, 32, 512), jn...  1.68 us

profile of v5, /device:TPU:4, one launch (start us, length us, event | category | flops | bytes accessed | tf_op | source)
XLA Modules:
  0.0 31.8 jit_solution(9168934173262563422)
XLA Ops:
  0.0 30.1 %parareal.1 = (f32[3,32,512]{2,1,0:T(8,128)}, f32[3,8,128]{2,1,0:T(8,128)}) custom-call(f32[3,32,512]{2,1,0:T(8,128)} %initial.1, f32[32,512]{1,0:T(8,128)} %rotation.1, s32[16]{0:T(128)} %flips.1), custom_call_target="tpu_custom_call" | custom-call | tf_op jit(solution)/shard_map/parareal/pallas_call | solution.py:464
  30.1 1.7 %finish.1 = f32[1,3,32,512]{3,2,1,0:T(8,128)} custom-call(f32[3,32,512]{2,1,0:T(8,128)} %get-tuple-element.7.fine, f32[3,8,128]{2,1,0:T(8,128)} %get-tuple-element.8.change), custom_call_target="tpu_custom_call" | custom-call | tf_op jit(solution)/shard_map/finish/pallas_call | solution.py:482

commit v6 on v5

--- a/solution.py
+++ b/solution.py
@@ -447,7 +447,7 @@
     dma = pltpu.SemaphoreType.DMA
     scratch = [
         vmem(3, 32, 512), vmem(32, 512),
-        vmem(3, 4, 32, 128), vmem(4, 32, 128),
+        vmem(3, 4, 40, 128), vmem(4, 40, 128),
         vmem(2, 3, 4, 16, 128), vmem(2, 4, 16, 128),
         vmem(3, 4, FR, 128), vmem(4, FR, 128), vmem(4, FR, 128),
         vmem(3, 4, 32, 128), vmem(2, 3, 4, 16, 128),

time: 32.3 us -> 32.3 us (level)
  no operation moved by 1% of the time
where the time goes in v6:
time: 32.3 us; the launch traced here: 31.8 us
  Pallas kernels  31.8 us (98%)
    pallas_call x1, Pallas kernels, body(): pl.pallas_call(kernel, out_shape=(jax.ShapeDtypeStruct((3, 32, 512), jnp....  30.1 us
    pallas_call x1, Pallas kernels, body(): pl.pallas_call(finish, out_shape=jax.ShapeDtypeStruct((1, 3, 32, 512), jn...  1.68 us

profile of v6, /device:TPU:4, one launch (start us, length us, event | category | flops | bytes accessed | tf_op | source)
XLA Modules:
  0.0 31.8 jit_solution(12656992941060519836)
XLA Ops:
  0.0 30.1 %parareal.1 = (f32[3,32,512]{2,1,0:T(8,128)}, f32[3,8,128]{2,1,0:T(8,128)}) custom-call(f32[3,32,512]{2,1,0:T(8,128)} %initial.1, f32[32,512]{1,0:T(8,128)} %rotation.1, s32[16]{0:T(128)} %flips.1), custom_call_target="tpu_custom_call" | custom-call | tf_op jit(solution)/shard_map/parareal/pallas_call | solution.py:464
  30.1 1.7 %finish.1 = f32[1,3,32,512]{3,2,1,0:T(8,128)} custom-call(f32[3,32,512]{2,1,0:T(8,128)} %get-tuple-element.7.fine, f32[3,8,128]{2,1,0:T(8,128)} %get-tuple-element.8.change), custom_call_target="tpu_custom_call" | custom-call | tf_op jit(solution)/shard_map/finish/pallas_call | solution.py:482
